TPU v7x, 512 devices: a whole 4x4x16 slice. The times are simulated.
512 devices in a mesh: tiles: 64 (over z, y), depth: 8 (over x, core).
Axes of the slice: x: 4, y: 4, z: 16, core: 2. Of those that a mesh axis runs over, the one named last changes fastest.
Arguments:
- thickness: float32 [16, 64, 128, 128], P('depth', 'tiles'), may hold values from 0.5 to 1.5
- u_layer: float32 [16, 64, 128, 128], P('depth', 'tiles'), may hold values from -4 to 4
- v_layer: float32 [16, 64, 128, 128], P('depth', 'tiles'), may hold values from -4 to 4
- tracers: float32 [6, 16, 64, 128, 128], P(None, 'depth', 'tiles'), may hold values from -6 to 6
- sea_level: float32 [64, 128, 128], P('tiles'), may hold values from -3 to 3
- u_column: float32 [64, 128, 128], P('tiles'), may hold values from -4 to 4
- v_column: float32 [64, 128, 128], P('tiles'), may hold values from -4 to 4
- wet_cells: int32 [64, 128, 128], P('tiles'), may hold values 0 or 1
- levels: int32 [64, 128, 128], P('tiles'), may hold values from 1 to 16
Outputs:
- tracers_new: float32 [6, 16, 64, 128, 128], P(None, 'depth', 'tiles')
- surface_new: float32 [64, 128, 128], P('tiles')
- east_new: float32 [64, 128, 128], P('tiles')
- north_new: float32 [64, 128, 128], P('tiles')
All inputs are finite; a program needn't handle non-finite values. No bound on the sum of `wet_cells` on one device may be relied on, other than what follows from the above.
Results may differ from a plain program's by a relative error of at most 0.0003.
Values sent between devices are 32-bit elements; how exact they have to be, the bound alone decides.
A program may use at most 64 MiB of HBM per device.

v0:
```python
import jax
import jax.numpy as jnp
from jax import lax
from jax.sharding import PartitionSpec as P

TROWS = 8
NSUB = 8


gravity = 1.0
substep_time = 0.45
tracer_time = 0.1


def shifted(value, axis, steps):
    count = lax.axis_size(axis)
    pairs = [(source, (source + steps) % count) for source in range(count)]
    return lax.ppermute(value, axis, pairs)


def from_behind(value, axis, by):
    peers = lax.axis_size(axis)
    pairs = [(i, i + by) for i in range(peers) if 0 <= i + by < peers]
    return lax.ppermute(value, axis, pairs)


def with_halo(value, sides, width):
    for axis, dim in sides:
        peers, length = (lax.axis_size(axis), value.shape[dim])
        up = [(i, (i + 1) % peers) for i in range(peers - 1)]
        down = [(j, i) for i, j in up]
        last = lax.slice_in_dim(value, length - width, length, axis=dim)
        leading = lax.slice_in_dim(value, 0, width, axis=dim)
        before = lax.ppermute(last, axis, up)
        after = lax.ppermute(leading, axis, down)
        value = jnp.concatenate([before, value, after], axis=dim)
    return value


def prefix(value, axis, combine, identity):
    peers, place = (lax.axis_size(axis), lax.axis_index(axis))
    everything = lax.all_gather(value, axis)
    start = jnp.broadcast_to(jnp.asarray(identity, value.dtype), value.shape)

    def step(k, before):
        at = peers - 1 - k
        reached = at > place
        new = combine(before, everything[at])
        return jnp.where(reached, new, before)

    return lax.fori_loop(0, peers, step, start)


def rim_cells(fields, rim_width):
    received = []
    for offset in (TROWS, -TROWS):
        if offset > 0:
            strip_part = fields[..., fields.shape[-1] - rim_width :]
        else:
            strip_part = fields[..., :rim_width]
        received.append(shifted(strip_part, "tiles", offset))
    widened = jnp.concatenate([received[0], fields, received[1]], axis=-1)
    tile_row = lax.axis_index("tiles") % TROWS
    arrived = []
    for offset in (1, -1):
        if offset > 0:
            strip_part = widened[..., widened.shape[-2] - rim_width :, :]
            edge_row = 0
        else:
            strip_part = widened[..., :rim_width, :]
            edge_row = TROWS - 1
        incoming = from_behind(strip_part, "tiles", offset)
        arrived.append(jnp.where(tile_row == edge_row, jnp.zeros_like(incoming), incoming))
    return jnp.concatenate([arrived[0], widened, arrived[1]], axis=-2)


def update_surface(surface, trans_east, trans_north, west_east, south_north, wet_tile):
    return surface - substep_time * wet_tile * (trans_east - west_east + trans_north - south_north)


def update_transport(
    transport, mask_face, depth_face, column_face, surface, beyond, coupling, layers_all
):
    return mask_face * (
        transport
        + substep_time
        * (-coupling * depth_face * (beyond - surface) + column_face / layers_all - transport)
    )


def body(thickness, u_layer, v_layer, tracers, sea_level, u_column, v_column, wet_cells, levels):
    layer_depth = thickness[:, 0]
    u_tile = u_layer[:, 0]
    v_tile = v_layer[:, 0]
    tracer_now = tracers[:, :, 0]
    layers_here = layer_depth.shape[0]
    layers_all = layers_here * lax.axis_size("depth")
    layer_ids = lax.axis_index("depth") * layers_here + jnp.arange(layers_here, dtype=jnp.int32)
    wet_tile = wet_cells[0].astype(jnp.float32)
    active = (layer_ids[:, None, None] < levels[0][None]).astype(jnp.float32) * wet_tile[None]
    padded = rim_cells(jnp.concatenate([layer_depth, active, wet_tile[None]], axis=0), 1)
    east_part = padded[:, 1:-1, 2:]
    north_part = padded[:, 2:, 1:-1]
    face_east = (
        0.5
        * (layer_depth + east_part[:layers_here])
        * (active * east_part[layers_here : 2 * layers_here])
    )
    face_north = (
        0.5
        * (layer_depth + north_part[:layers_here])
        * (active * north_part[layers_here : 2 * layers_here])
    )
    flux_east = u_tile * face_east
    flux_north = v_tile * face_north
    wet_east = wet_tile * east_part[2 * layers_here]
    wet_north = wet_tile * north_part[2 * layers_here]
    column_east, column_north, depth_east, depth_north = lax.psum(
        (
            jnp.sum(flux_east, axis=0),
            jnp.sum(flux_north, axis=0),
            jnp.sum(face_east, axis=0),
            jnp.sum(face_north, axis=0),
        ),
        "depth",
    )
    coupling = gravity / layers_all
    surface = sea_level[0]
    trans_east = u_column[0]
    trans_north = v_column[0]
    for substep in range(NSUB):
        framed = rim_cells(jnp.stack([trans_east, trans_north]), 1)
        surface = update_surface(
            surface, trans_east, trans_north, framed[0, 1:-1, :-2], framed[1, :-2, 1:-1], wet_tile
        )
        framed_surface = rim_cells(surface[None], 1)[0]
        trans_east = update_transport(
            trans_east,
            wet_east,
            depth_east,
            column_east,
            surface,
            framed_surface[1:-1, 2:],
            coupling,
            layers_all,
        )
        trans_north = update_transport(
            trans_north,
            wet_north,
            depth_north,
            column_north,
            surface,
            framed_surface[2:, 1:-1],
            coupling,
            layers_all,
        )
    final_east = flux_east + face_east * (trans_east - column_east / layers_all)[None]
    final_north = flux_north + face_north * (trans_north - column_north / layers_all)[None]
    species = tracer_now.shape[0]
    rows_here = tracer_now.shape[2]
    cols_here = tracer_now.shape[3]
    vertical = with_halo(tracer_now, (("depth", 1),), 1)
    stacked = jnp.concatenate(
        [tracer_now.reshape(species * layers_here, rows_here, cols_here), final_east, final_north],
        axis=0,
    )
    framed_all = rim_cells(stacked, 1)
    tracer_wide = framed_all[: species * layers_here].reshape(
        species, layers_here, rows_here + 2, cols_here + 2
    )
    east_wide = framed_all[species * layers_here : species * layers_here + layers_here]
    north_wide = framed_all[species * layers_here + layers_here :]
    east_faces = east_wide[:, 1:-1, :-1]
    side_east = (
        jnp.maximum(east_faces, 0.0) * tracer_wide[:, :, 1:-1, :-1]
        + jnp.minimum(east_faces, 0.0) * tracer_wide[:, :, 1:-1, 1:]
    )
    north_faces = north_wide[:, :-1, 1:-1]
    side_north = (
        jnp.maximum(north_faces, 0.0) * tracer_wide[:, :, :-1, 1:-1]
        + jnp.minimum(north_faces, 0.0) * tracer_wide[:, :, 1:, 1:-1]
    )
    divergence = final_east - east_wide[:, 1:-1, :-2] + final_north - north_wide[:, :-2, 1:-1]
    local_total = jnp.sum(divergence, axis=0)
    deeper = prefix(local_total, "depth", jnp.add, jnp.zeros_like(local_total))
    suffix = jnp.cumsum(divergence[::-1], axis=0)[::-1] + deeper[None]
    lift_bottom = divergence - suffix
    lift_top = jnp.where(layer_ids[:, None, None] == 0, 0.0, -suffix)
    tracer_above = vertical[:, :-2]
    tracer_below = vertical[:, 2:]
    vert_bottom = (
        jnp.maximum(lift_bottom, 0.0) * tracer_below + jnp.minimum(lift_bottom, 0.0) * tracer_now
    )
    vert_top = jnp.maximum(lift_top, 0.0) * tracer_now + jnp.minimum(lift_top, 0.0) * tracer_above
    horizontal = (
        side_east[..., 1:] - side_east[..., :-1] + side_north[..., 1:, :] - side_north[..., :-1, :]
    )
    tendency = -horizontal + vert_bottom - vert_top
    updated = tracer_now + tracer_time * active * tendency / layer_depth
    return (updated[:, :, None], surface[None], trans_east[None], trans_north[None])


def solution(mesh):
    return jax.shard_map(
        body,
        mesh=mesh,
        in_specs=(
            P("depth", "tiles", None, None),
            P("depth", "tiles", None, None),
            P("depth", "tiles", None, None),
            P(None, "depth", "tiles", None, None),
            P("tiles", None, None),
            P("tiles", None, None),
            P("tiles", None, None),
            P("tiles", None, None),
            P("tiles", None, None),
        ),
        out_specs=(
            P(None, "depth", "tiles", None, None),
            P("tiles", None, None),
            P("tiles", None, None),
            P("tiles", None, None),
        ),
        check_vma=False,
    )
```

profile of v0, /device:TPU:1, one launch (start us, length us, event | category | flops | bytes accessed | tf_op | source)
XLA Modules:
  0.0 508.1 jit_solution(5844324518921240593)
XLA Ops:
  9.0 12.4 %collective-permute-start.2 = (f32[2,128,1]{2,1,0:T(8,128)S(1)}, f32[2,128,1]{2,1,0:T(8,128)S(1)}, u32[]{:S(2)}, u32[]{:S(2)}) collective-permute-start(f32[2,128,1]{2,1,0:T(8,128)S(1)} %get-tuple-element.234), channel_id=1, source_target_pairs={{0,448},{8,456},{16,464},{24,472},{32,480},{40,488},{48,496},{56,5... | collective-permute-start | bytes 3080 | tf_op jit(solution)/shard_map/ppermute | solution.py:18
  29.1 5.5 %collective-permute-start = (f32[5,128,1]{2,1,0:T(8,128)S(1)}, f32[5,128,1]{2,1,0:T(8,128)S(1)}, u32[]{:S(2)}, u32[]{:S(2)}) collective-permute-start(f32[5,128,1]{2,1,0:T(8,128)S(1)} %get-tuple-element.185), channel_id=1, source_target_pairs={{0,448},{8,456},{16,464},{24,472},{32,480},{40,488},{48,496},{56,5... | collective-permute-start | bytes 7688 | tf_op jit(solution)/shard_map/ppermute | solution.py:18
  38.8 9.6 %collective-permute-start.4 = (f32[1,128,1]{2,1,0:T(8,128)S(1)}, f32[1,128,1]{2,1,0:T(8,128)S(1)}, u32[]{:S(2)}, u32[]{:S(2)}) collective-permute-start(f32[1,128,1]{2,1,0:T(8,128)S(1)} %get-tuple-element.250), channel_id=1, source_target_pairs={{0,64},{8,72},{16,80},{24,88},{32,96},{40,104},{48,112},{56,120},{... | collective-permute-start | bytes 1544 | tf_op jit(solution)/shard_map/ppermute | solution.py:18
  48.3 6.9 %collective-permute-start.5 = (f32[1,128,1]{2,1,0:T(8,128)S(1)}, f32[1,128,1]{2,1,0:T(8,128)S(1)}, u32[]{:S(2)}, u32[]{:S(2)}) collective-permute-start(f32[1,128,1]{2,1,0:T(8,128)S(1)} %get-tuple-element.251), channel_id=1, source_target_pairs={{0,448},{8,456},{16,464},{24,472},{32,480},{40,488},{48,496},{56,5... | collective-permute-start | bytes 1544 | tf_op jit(solution)/shard_map/ppermute | solution.py:18
  56.8 4.0 collective-permute-start.6
  66.1 73.9 %all-reduce.3.cloned.1.call-done = (f32[128,128]{1,0:T(8,128)}, f32[128,128]{1,0:T(8,128)}, f32[128,128]{1,0:T(8,128)}, f32[128,128]{1,0:T(8,128)}) async-done(((f32[128,128]{1,0:T(8,128)}, f32[128,128]{1,0:T(8,128)}, f32[128,128]{1,0:T(8,128)}, f32[128,128]{1,0:T(8,128)}), (f32[128,128]{1,0:T(8,128)}, f32[128,128]{1,0:T(8,128)}, f32[128,128]{1,0:T(8,128)}, ...) | async-done | bytes 262160 | tf_op jit(solution)/shard_map/psum | solution.py:118
  145.7 4.2 collective-permute-start.11
  159.0 8.0 %collective-permute-start.13 = (f32[1,128,1]{2,1,0:T(8,128)S(1)}, f32[1,128,1]{2,1,0:T(8,128)S(1)}, u32[]{:S(2)}, u32[]{:S(2)}) collective-permute-start(f32[1,128,1]{2,1,0:T(8,128)S(1)} %get-tuple-element.248), channel_id=1, source_target_pairs={{0,64},{8,72},{16,80},{24,88},{32,96},{40,104},{48,112},{56,120},{... | collective-permute-start | bytes 1544 | tf_op jit(solution)/shard_map/ppermute | solution.py:18
  169.0 5.0 collective-permute-done.14
  180.1 8.0 %collective-permute-start.17 = (f32[2,128,1]{2,1,0:T(8,128)S(1)}, f32[2,128,1]{2,1,0:T(8,128)S(1)}, u32[]{:S(2)}, u32[]{:S(2)}) collective-permute-start(f32[2,128,1]{2,1,0:T(8,128)S(1)} %get-tuple-element.230), channel_id=1, source_target_pairs={{0,64},{8,72},{16,80},{24,88},{32,96},{40,104},{48,112},{56,120},{... | collective-permute-start | bytes 3080 | tf_op jit(solution)/shard_map/ppermute | solution.py:18
  190.0 5.1 %collective-permute-done.18 = f32[2,128,1]{2,1,0:T(8,128)S(1)} collective-permute-done((f32[2,128,1]{2,1,0:T(8,128)S(1)}, f32[2,128,1]{2,1,0:T(8,128)S(1)}, u32[]{:S(2)}, u32[]{:S(2)}) %collective-permute-start.18) | collective-permute-done | bytes 1056 | tf_op jit(solution)/shard_map/ppermute | solution.py:18
  197.4 9.9 %collective-permute-start.20 = (f32[1,128,1]{2,1,0:T(8,128)S(1)}, f32[1,128,1]{2,1,0:T(8,128)S(1)}, u32[]{:S(2)}, u32[]{:S(2)}) collective-permute-start(f32[1,128,1]{2,1,0:T(8,128)S(1)} %get-tuple-element.246), channel_id=1, source_target_pairs={{0,64},{8,72},{16,80},{24,88},{32,96},{40,104},{48,112},{56,120},{... | collective-permute-start | bytes 1544 | tf_op jit(solution)/shard_map/ppermute | solution.py:18
  209.2 4.8 collective-permute-done.21
  220.0 7.3 %collective-permute-start.24 = (f32[2,128,1]{2,1,0:T(8,128)S(1)}, f32[2,128,1]{2,1,0:T(8,128)S(1)}, u32[]{:S(2)}, u32[]{:S(2)}) collective-permute-start(f32[2,128,1]{2,1,0:T(8,128)S(1)} %get-tuple-element.228), channel_id=1, source_target_pairs={{0,64},{8,72},{16,80},{24,88},{32,96},{40,104},{48,112},{56,120},{... | collective-permute-start | bytes 3080 | tf_op jit(solution)/shard_map/ppermute | solution.py:18
  229.8 4.2 collective-permute-done.25
  236.3 8.4 %collective-permute-start.27 = (f32[1,128,1]{2,1,0:T(8,128)S(1)}, f32[1,128,1]{2,1,0:T(8,128)S(1)}, u32[]{:S(2)}, u32[]{:S(2)}) collective-permute-start(f32[1,128,1]{2,1,0:T(8,128)S(1)} %get-tuple-element.244), channel_id=1, source_target_pairs={{0,64},{8,72},{16,80},{24,88},{32,96},{40,104},{48,112},{56,120},{... | collective-permute-start | bytes 1544 | tf_op jit(solution)/shard_map/ppermute | solution.py:18
  244.7 3.8 collective-permute-start.28
  256.7 7.5 %collective-permute-start.31 = (f32[2,128,1]{2,1,0:T(8,128)S(1)}, f32[2,128,1]{2,1,0:T(8,128)S(1)}, u32[]{:S(2)}, u32[]{:S(2)}) collective-permute-start(f32[2,128,1]{2,1,0:T(8,128)S(1)} %get-tuple-element.226), channel_id=1, source_target_pairs={{0,64},{8,72},{16,80},{24,88},{32,96},{40,104},{48,112},{56,120},{... | collective-permute-start | bytes 3080 | tf_op jit(solution)/shard_map/ppermute | solution.py:18
  273.0 8.4 %collective-permute-start.34 = (f32[1,128,1]{2,1,0:T(8,128)S(1)}, f32[1,128,1]{2,1,0:T(8,128)S(1)}, u32[]{:S(2)}, u32[]{:S(2)}) collective-permute-start(f32[1,128,1]{2,1,0:T(8,128)S(1)} %get-tuple-element.242), channel_id=1, source_target_pairs={{0,64},{8,72},{16,80},{24,88},{32,96},{40,104},{48,112},{56,120},{... | collective-permute-start | bytes 1544 | tf_op jit(solution)/shard_map/ppermute | solution.py:18
  293.4 7.2 %collective-permute-start.38 = (f32[2,128,1]{2,1,0:T(8,128)S(1)}, f32[2,128,1]{2,1,0:T(8,128)S(1)}, u32[]{:S(2)}, u32[]{:S(2)}) collective-permute-start(f32[2,128,1]{2,1,0:T(8,128)S(1)} %get-tuple-element.224), channel_id=1, source_target_pairs={{0,64},{8,72},{16,80},{24,88},{32,96},{40,104},{48,112},{56,120},{... | collective-permute-start | bytes 3080 | tf_op jit(solution)/shard_map/ppermute | solution.py:18
  310.9 9.2 %collective-permute-start.41 = (f32[1,128,1]{2,1,0:T(8,128)S(1)}, f32[1,128,1]{2,1,0:T(8,128)S(1)}, u32[]{:S(2)}, u32[]{:S(2)}) collective-permute-start(f32[1,128,1]{2,1,0:T(8,128)S(1)} %get-tuple-element.240), channel_id=1, source_target_pairs={{0,64},{8,72},{16,80},{24,88},{32,96},{40,104},{48,112},{56,120},{... | collective-permute-start | bytes 1544 | tf_op jit(solution)/shard_map/ppermute | solution.py:18
  322.0 6.1 %collective-permute-done.42 = f32[1,128,1]{2,1,0:T(8,128)S(1)} collective-permute-done((f32[1,128,1]{2,1,0:T(8,128)S(1)}, f32[1,128,1]{2,1,0:T(8,128)S(1)}, u32[]{:S(2)}, u32[]{:S(2)}) %collective-permute-start.42) | collective-permute-done | bytes 544 | tf_op jit(solution)/shard_map/ppermute | solution.py:18
  334.1 7.0 %collective-permute-start.45 = (f32[2,128,1]{2,1,0:T(8,128)S(1)}, f32[2,128,1]{2,1,0:T(8,128)S(1)}, u32[]{:S(2)}, u32[]{:S(2)}) collective-permute-start(f32[2,128,1]{2,1,0:T(8,128)S(1)} %get-tuple-element.222), channel_id=1, source_target_pairs={{0,64},{8,72},{16,80},{24,88},{32,96},{40,104},{48,112},{56,120},{... | collective-permute-start | bytes 3080 | tf_op jit(solution)/shard_map/ppermute | solution.py:18
  343.7 4.7 collective-permute-done.46
  350.7 9.2 %collective-permute-start.48 = (f32[1,128,1]{2,1,0:T(8,128)S(1)}, f32[1,128,1]{2,1,0:T(8,128)S(1)}, u32[]{:S(2)}, u32[]{:S(2)}) collective-permute-start(f32[1,128,1]{2,1,0:T(8,128)S(1)} %get-tuple-element.238), channel_id=1, source_target_pairs={{0,64},{8,72},{16,80},{24,88},{32,96},{40,104},{48,112},{56,120},{... | collective-permute-start | bytes 1544 | tf_op jit(solution)/shard_map/ppermute | solution.py:18
  362.0 5.9 %collective-permute-done.49 = f32[1,128,1]{2,1,0:T(8,128)S(1)} collective-permute-done((f32[1,128,1]{2,1,0:T(8,128)S(1)}, f32[1,128,1]{2,1,0:T(8,128)S(1)}, u32[]{:S(2)}, u32[]{:S(2)}) %collective-permute-start.49) | collective-permute-done | bytes 544 | tf_op jit(solution)/shard_map/ppermute | solution.py:18
  374.0 7.8 %collective-permute-start.52 = (f32[2,128,1]{2,1,0:T(8,128)S(1)}, f32[2,128,1]{2,1,0:T(8,128)S(1)}, u32[]{:S(2)}, u32[]{:S(2)}) collective-permute-start(f32[2,128,1]{2,1,0:T(8,128)S(1)} %get-tuple-element.220), channel_id=1, source_target_pairs={{0,64},{8,72},{16,80},{24,88},{32,96},{40,104},{48,112},{56,120},{... | collective-permute-start | bytes 3080 | tf_op jit(solution)/shard_map/ppermute | solution.py:18
  383.7 5.0 collective-permute-done.53
  390.9 8.0 %collective-permute-start.55 = (f32[1,128,1]{2,1,0:T(8,128)S(1)}, f32[1,128,1]{2,1,0:T(8,128)S(1)}, u32[]{:S(2)}, u32[]{:S(2)}) collective-permute-start(f32[1,128,1]{2,1,0:T(8,128)S(1)} %get-tuple-element.236), channel_id=1, source_target_pairs={{0,64},{8,72},{16,80},{24,88},{32,96},{40,104},{48,112},{56,120},{... | collective-permute-start | bytes 1544 | tf_op jit(solution)/shard_map/ppermute | solution.py:18
  407.2 37.7 %collective-permute-start.63 = (f32[6,1,128,128]{3,2,1,0:T(8,128)}, f32[6,1,128,128]{3,2,1,0:T(8,128)}, u32[]{:S(2)}, u32[]{:S(2)}) collective-permute-start(f32[6,1,128,128]{3,2,1,0:T(8,128)} %get-tuple-element.180), channel_id=1, source_target_pairs={{1,0},{2,1},{3,2},{4,3},{5,4},{6,5},{7,6},{9,8},{10,9},{11,10},{12... | collective-permute-start | bytes 1179656 | tf_op jit(solution)/shard_map/ppermute | solution.py:35
  452.9 7.1 %collective-permute-start.59 = (f32[16,128,1]{1,0,2:T(8,128)S(1)}, f32[16,128,1]{1,0,2:T(8,128)S(1)}, u32[]{:S(2)}, u32[]{:S(2)}) collective-permute-start(f32[16,128,1]{1,0,2:T(8,128)S(1)} %copy.53), channel_id=1, source_target_pairs={{0,64},{8,72},{16,80},{24,88},{32,96},{40,104},{48,112},{56,120},{... | collective-permute-start | bytes 24584 | tf_op jit(solution)/shard_map/ppermute | solution.py:18
  476.7 17.9 %all-gather = f32[1024,128]{1,0:T(8,128)S(1)} all-gather(f32[128,128]{1,0:T(8,128)S(1)} %get-tuple-element.156), channel_id=2, replica_groups=mesh['tiles'=64,'depth'=8] {'depth'}, dimensions={0}, use_global_device_ids=true | all-gather | bytes 589824 | tf_op jit(solution)/shard_map/all_gather | solution.py:42
  (270 shorter events, 163.2 us)
Async XLA Ops:
  7.2 132.8 %all-reduce.3.cloned.1.call-start = ((), (), s32[]{:S(2)}) async-start(), calls=%async_computation | async-start | bytes 524288 | tf_op jit(solution)/shard_map/psum | solution.py:118
  9.0 25.5 %collective-permute-start.2 = (f32[2,128,1]{2,1,0:T(8,128)S(1)}, f32[2,128,1]{2,1,0:T(8,128)S(1)}, u32[]{:S(2)}, u32[]{:S(2)}) collective-permute-start(f32[2,128,1]{2,1,0:T(8,128)S(1)} %get-tuple-element.234), channel_id=1, source_target_pairs={{0,448},{8,456},{16,464},{24,472},{32,480},{40,488},{48,496},{56,5... | collective-permute-start | bytes 3080 | tf_op jit(solution)/shard_map/ppermute | solution.py:18
  21.4 13.1 %collective-permute-start.1 = (f32[2,128,1]{2,1,0:T(8,128)S(1)}, f32[2,128,1]{2,1,0:T(8,128)S(1)}, u32[]{:S(2)}, u32[]{:S(2)}) collective-permute-start(f32[2,128,1]{2,1,0:T(8,128)S(1)} %get-tuple-element.235), channel_id=1, source_target_pairs={{0,64},{8,72},{16,80},{24,88},{32,96},{40,104},{48,112},{56,120},{... | collective-permute-start | bytes 3080 | tf_op jit(solution)/shard_map/ppermute | solution.py:18
  27.0 28.3 %collective-permute-start.8 = (f32[5,128,1]{2,1,0:T(8,128)S(1)}, f32[5,128,1]{2,1,0:T(8,128)S(1)}, u32[]{:S(2)}, u32[]{:S(2)}) collective-permute-start(f32[5,128,1]{2,1,0:T(8,128)S(1)} %get-tuple-element.184), channel_id=1, source_target_pairs={{0,64},{8,72},{16,80},{24,88},{32,96},{40,104},{48,112},{56,120},{... | collective-permute-start | bytes 7688 | tf_op jit(solution)/shard_map/ppermute | solution.py:18
  29.1 26.2 %collective-permute-start = (f32[5,128,1]{2,1,0:T(8,128)S(1)}, f32[5,128,1]{2,1,0:T(8,128)S(1)}, u32[]{:S(2)}, u32[]{:S(2)}) collective-permute-start(f32[5,128,1]{2,1,0:T(8,128)S(1)} %get-tuple-element.185), channel_id=1, source_target_pairs={{0,448},{8,456},{16,464},{24,472},{32,480},{40,488},{48,496},{56,5... | collective-permute-start | bytes 7688 | tf_op jit(solution)/shard_map/ppermute | solution.py:18
  38.8 17.9 %collective-permute-start.4 = (f32[1,128,1]{2,1,0:T(8,128)S(1)}, f32[1,128,1]{2,1,0:T(8,128)S(1)}, u32[]{:S(2)}, u32[]{:S(2)}) collective-permute-start(f32[1,128,1]{2,1,0:T(8,128)S(1)} %get-tuple-element.250), channel_id=1, source_target_pairs={{0,64},{8,72},{16,80},{24,88},{32,96},{40,104},{48,112},{56,120},{... | collective-permute-start | bytes 1544 | tf_op jit(solution)/shard_map/ppermute | solution.py:18
  48.3 8.4 %collective-permute-start.5 = (f32[1,128,1]{2,1,0:T(8,128)S(1)}, f32[1,128,1]{2,1,0:T(8,128)S(1)}, u32[]{:S(2)}, u32[]{:S(2)}) collective-permute-start(f32[1,128,1]{2,1,0:T(8,128)S(1)} %get-tuple-element.251), channel_id=1, source_target_pairs={{0,448},{8,456},{16,464},{24,472},{32,480},{40,488},{48,496},{56,5... | collective-permute-start | bytes 1544 | tf_op jit(solution)/shard_map/ppermute | solution.py:18
  55.4 7.6 %collective-permute-start.9 = (f32[5,1,130]{2,1,0:T(1,128)S(1)}, f32[5,1,130]{2,1,0:T(1,128)S(1)}, u32[]{:S(2)}, u32[]{:S(2)}) collective-permute-start(f32[5,1,130]{2,1,0:T(1,128)S(1)} %pad_maximum_fusion.86), channel_id=1, source_target_pairs={{8,0},{16,8},{24,16},{32,24},{40,32},{48,40},{56,48},{64,56},{72,6... | collective-permute-start | bytes 7808 | tf_op jit(solution)/shard_map/ppermute | solution.py:24
  142.2 9.2 %collective-permute-start.10 = (f32[2,128,1]{2,1,0:T(8,128)S(1)}, f32[2,128,1]{2,1,0:T(8,128)S(1)}, u32[]{:S(2)}, u32[]{:S(2)}) collective-permute-start(f32[2,128,1]{2,1,0:T(8,128)S(1)} %get-tuple-element.232), channel_id=1, source_target_pairs={{0,64},{8,72},{16,80},{24,88},{32,96},{40,104},{48,112},{56,120},{... | collective-permute-start | bytes 3080 | tf_op jit(solution)/shard_map/ppermute | solution.py:18
  145.7 9.2 %collective-permute-start.11 = (f32[2,128,1]{2,1,0:T(8,128)S(1)}, f32[2,128,1]{2,1,0:T(8,128)S(1)}, u32[]{:S(2)}, u32[]{:S(2)}) collective-permute-start(f32[2,128,1]{2,1,0:T(8,128)S(1)} %get-tuple-element.233), channel_id=1, source_target_pairs={{0,448},{8,456},{16,464},{24,472},{32,480},{40,488},{48,496},{56,5... | collective-permute-start | bytes 3080 | tf_op jit(solution)/shard_map/ppermute | solution.py:18
  159.0 10.0 %collective-permute-start.13 = (f32[1,128,1]{2,1,0:T(8,128)S(1)}, f32[1,128,1]{2,1,0:T(8,128)S(1)}, u32[]{:S(2)}, u32[]{:S(2)}) collective-permute-start(f32[1,128,1]{2,1,0:T(8,128)S(1)} %get-tuple-element.248), channel_id=1, source_target_pairs={{0,64},{8,72},{16,80},{24,88},{32,96},{40,104},{48,112},{56,120},{... | collective-permute-start | bytes 1544 | tf_op jit(solution)/shard_map/ppermute | solution.py:18
  180.1 9.9 %collective-permute-start.17 = (f32[2,128,1]{2,1,0:T(8,128)S(1)}, f32[2,128,1]{2,1,0:T(8,128)S(1)}, u32[]{:S(2)}, u32[]{:S(2)}) collective-permute-start(f32[2,128,1]{2,1,0:T(8,128)S(1)} %get-tuple-element.230), channel_id=1, source_target_pairs={{0,64},{8,72},{16,80},{24,88},{32,96},{40,104},{48,112},{56,120},{... | collective-permute-start | bytes 3080 | tf_op jit(solution)/shard_map/ppermute | solution.py:18
  188.0 7.0 %collective-permute-start.18 = (f32[2,128,1]{2,1,0:T(8,128)S(1)}, f32[2,128,1]{2,1,0:T(8,128)S(1)}, u32[]{:S(2)}, u32[]{:S(2)}) collective-permute-start(f32[2,128,1]{2,1,0:T(8,128)S(1)} %get-tuple-element.231), channel_id=1, source_target_pairs={{0,448},{8,456},{16,464},{24,472},{32,480},{40,488},{48,496},{56,5... | collective-permute-start | bytes 3080 | tf_op jit(solution)/shard_map/ppermute | solution.py:18
  197.4 11.8 %collective-permute-start.20 = (f32[1,128,1]{2,1,0:T(8,128)S(1)}, f32[1,128,1]{2,1,0:T(8,128)S(1)}, u32[]{:S(2)}, u32[]{:S(2)}) collective-permute-start(f32[1,128,1]{2,1,0:T(8,128)S(1)} %get-tuple-element.246), channel_id=1, source_target_pairs={{0,64},{8,72},{16,80},{24,88},{32,96},{40,104},{48,112},{56,120},{... | collective-permute-start | bytes 1544 | tf_op jit(solution)/shard_map/ppermute | solution.py:18
  220.0 9.8 %collective-permute-start.24 = (f32[2,128,1]{2,1,0:T(8,128)S(1)}, f32[2,128,1]{2,1,0:T(8,128)S(1)}, u32[]{:S(2)}, u32[]{:S(2)}) collective-permute-start(f32[2,128,1]{2,1,0:T(8,128)S(1)} %get-tuple-element.228), channel_id=1, source_target_pairs={{0,64},{8,72},{16,80},{24,88},{32,96},{40,104},{48,112},{56,120},{... | collective-permute-start | bytes 3080 | tf_op jit(solution)/shard_map/ppermute | solution.py:18
  236.3 12.3 %collective-permute-start.27 = (f32[1,128,1]{2,1,0:T(8,128)S(1)}, f32[1,128,1]{2,1,0:T(8,128)S(1)}, u32[]{:S(2)}, u32[]{:S(2)}) collective-permute-start(f32[1,128,1]{2,1,0:T(8,128)S(1)} %get-tuple-element.244), channel_id=1, source_target_pairs={{0,64},{8,72},{16,80},{24,88},{32,96},{40,104},{48,112},{56,120},{... | collective-permute-start | bytes 1544 | tf_op jit(solution)/shard_map/ppermute | solution.py:18
  256.7 11.1 %collective-permute-start.31 = (f32[2,128,1]{2,1,0:T(8,128)S(1)}, f32[2,128,1]{2,1,0:T(8,128)S(1)}, u32[]{:S(2)}, u32[]{:S(2)}) collective-permute-start(f32[2,128,1]{2,1,0:T(8,128)S(1)} %get-tuple-element.226), channel_id=1, source_target_pairs={{0,64},{8,72},{16,80},{24,88},{32,96},{40,104},{48,112},{56,120},{... | collective-permute-start | bytes 3080 | tf_op jit(solution)/shard_map/ppermute | solution.py:18
  273.0 12.5 %collective-permute-start.34 = (f32[1,128,1]{2,1,0:T(8,128)S(1)}, f32[1,128,1]{2,1,0:T(8,128)S(1)}, u32[]{:S(2)}, u32[]{:S(2)}) collective-permute-start(f32[1,128,1]{2,1,0:T(8,128)S(1)} %get-tuple-element.242), channel_id=1, source_target_pairs={{0,64},{8,72},{16,80},{24,88},{32,96},{40,104},{48,112},{56,120},{... | collective-permute-start | bytes 1544 | tf_op jit(solution)/shard_map/ppermute | solution.py:18
  293.4 11.9 %collective-permute-start.38 = (f32[2,128,1]{2,1,0:T(8,128)S(1)}, f32[2,128,1]{2,1,0:T(8,128)S(1)}, u32[]{:S(2)}, u32[]{:S(2)}) collective-permute-start(f32[2,128,1]{2,1,0:T(8,128)S(1)} %get-tuple-element.224), channel_id=1, source_target_pairs={{0,64},{8,72},{16,80},{24,88},{32,96},{40,104},{48,112},{56,120},{... | collective-permute-start | bytes 3080 | tf_op jit(solution)/shard_map/ppermute | solution.py:18
  300.6 7.3 %collective-permute-start.39 = (f32[2,128,1]{2,1,0:T(8,128)S(1)}, f32[2,128,1]{2,1,0:T(8,128)S(1)}, u32[]{:S(2)}, u32[]{:S(2)}) collective-permute-start(f32[2,128,1]{2,1,0:T(8,128)S(1)} %get-tuple-element.225), channel_id=1, source_target_pairs={{0,448},{8,456},{16,464},{24,472},{32,480},{40,488},{48,496},{56,5... | collective-permute-start | bytes 3080 | tf_op jit(solution)/shard_map/ppermute | solution.py:18
  310.9 11.1 %collective-permute-start.41 = (f32[1,128,1]{2,1,0:T(8,128)S(1)}, f32[1,128,1]{2,1,0:T(8,128)S(1)}, u32[]{:S(2)}, u32[]{:S(2)}) collective-permute-start(f32[1,128,1]{2,1,0:T(8,128)S(1)} %get-tuple-element.240), channel_id=1, source_target_pairs={{0,64},{8,72},{16,80},{24,88},{32,96},{40,104},{48,112},{56,120},{... | collective-permute-start | bytes 1544 | tf_op jit(solution)/shard_map/ppermute | solution.py:18
  320.0 8.1 %collective-permute-start.42 = (f32[1,128,1]{2,1,0:T(8,128)S(1)}, f32[1,128,1]{2,1,0:T(8,128)S(1)}, u32[]{:S(2)}, u32[]{:S(2)}) collective-permute-start(f32[1,128,1]{2,1,0:T(8,128)S(1)} %get-tuple-element.241), channel_id=1, source_target_pairs={{0,448},{8,456},{16,464},{24,472},{32,480},{40,488},{48,496},{56,5... | collective-permute-start | bytes 1544 | tf_op jit(solution)/shard_map/ppermute | solution.py:18
  334.1 9.6 %collective-permute-start.45 = (f32[2,128,1]{2,1,0:T(8,128)S(1)}, f32[2,128,1]{2,1,0:T(8,128)S(1)}, u32[]{:S(2)}, u32[]{:S(2)}) collective-permute-start(f32[2,128,1]{2,1,0:T(8,128)S(1)} %get-tuple-element.222), channel_id=1, source_target_pairs={{0,64},{8,72},{16,80},{24,88},{32,96},{40,104},{48,112},{56,120},{... | collective-permute-start | bytes 3080 | tf_op jit(solution)/shard_map/ppermute | solution.py:18
  341.1 7.3 %collective-permute-start.46 = (f32[2,128,1]{2,1,0:T(8,128)S(1)}, f32[2,128,1]{2,1,0:T(8,128)S(1)}, u32[]{:S(2)}, u32[]{:S(2)}) collective-permute-start(f32[2,128,1]{2,1,0:T(8,128)S(1)} %get-tuple-element.223), channel_id=1, source_target_pairs={{0,448},{8,456},{16,464},{24,472},{32,480},{40,488},{48,496},{56,5... | collective-permute-start | bytes 3080 | tf_op jit(solution)/shard_map/ppermute | solution.py:18
  350.7 11.3 %collective-permute-start.48 = (f32[1,128,1]{2,1,0:T(8,128)S(1)}, f32[1,128,1]{2,1,0:T(8,128)S(1)}, u32[]{:S(2)}, u32[]{:S(2)}) collective-permute-start(f32[1,128,1]{2,1,0:T(8,128)S(1)} %get-tuple-element.238), channel_id=1, source_target_pairs={{0,64},{8,72},{16,80},{24,88},{32,96},{40,104},{48,112},{56,120},{... | collective-permute-start | bytes 1544 | tf_op jit(solution)/shard_map/ppermute | solution.py:18
  360.0 8.0 %collective-permute-start.49 = (f32[1,128,1]{2,1,0:T(8,128)S(1)}, f32[1,128,1]{2,1,0:T(8,128)S(1)}, u32[]{:S(2)}, u32[]{:S(2)}) collective-permute-start(f32[1,128,1]{2,1,0:T(8,128)S(1)} %get-tuple-element.239), channel_id=1, source_target_pairs={{0,448},{8,456},{16,464},{24,472},{32,480},{40,488},{48,496},{56,5... | collective-permute-start | bytes 1544 | tf_op jit(solution)/shard_map/ppermute | solution.py:18
  374.0 9.7 %collective-permute-start.52 = (f32[2,128,1]{2,1,0:T(8,128)S(1)}, f32[2,128,1]{2,1,0:T(8,128)S(1)}, u32[]{:S(2)}, u32[]{:S(2)}) collective-permute-start(f32[2,128,1]{2,1,0:T(8,128)S(1)} %get-tuple-element.220), channel_id=1, source_target_pairs={{0,64},{8,72},{16,80},{24,88},{32,96},{40,104},{48,112},{56,120},{... | collective-permute-start | bytes 3080 | tf_op jit(solution)/shard_map/ppermute | solution.py:18
  390.9 10.6 %collective-permute-start.55 = (f32[1,128,1]{2,1,0:T(8,128)S(1)}, f32[1,128,1]{2,1,0:T(8,128)S(1)}, u32[]{:S(2)}, u32[]{:S(2)}) collective-permute-start(f32[1,128,1]{2,1,0:T(8,128)S(1)} %get-tuple-element.236), channel_id=1, source_target_pairs={{0,64},{8,72},{16,80},{24,88},{32,96},{40,104},{48,112},{56,120},{... | collective-permute-start | bytes 1544 | tf_op jit(solution)/shard_map/ppermute | solution.py:18
  405.0 43.1 %collective-permute-start.57 = (f32[1,1,130]{2,1,0:T(1,128)S(1)}, f32[1,1,130]{2,1,0:T(1,128)S(1)}, u32[]{:S(2)}, u32[]{:S(2)}) collective-permute-start(f32[1,1,130]{2,1,0:T(1,128)S(1)} %get-tuple-element.204), channel_id=1, source_target_pairs={{0,8},{8,16},{16,24},{24,32},{32,40},{40,48},{48,56},{56,64},{64,7... | collective-permute-start | bytes 1568 | tf_op jit(solution)/shard_map/ppermute | solution.py:24
  407.2 91.2 %collective-permute-start.63 = (f32[6,1,128,128]{3,2,1,0:T(8,128)}, f32[6,1,128,128]{3,2,1,0:T(8,128)}, u32[]{:S(2)}, u32[]{:S(2)}) collective-permute-start(f32[6,1,128,128]{3,2,1,0:T(8,128)} %get-tuple-element.180), channel_id=1, source_target_pairs={{1,0},{2,1},{3,2},{4,3},{5,4},{6,5},{7,6},{9,8},{10,9},{11,10},{12... | collective-permute-start | bytes 1179656 | tf_op jit(solution)/shard_map/ppermute | solution.py:35
  444.9 53.6 %collective-permute-start.64 = (f32[6,1,128,128]{3,2,1,0:T(8,128)}, f32[6,1,128,128]{3,2,1,0:T(8,128)}, u32[]{:S(2)}, u32[]{:S(2)}) collective-permute-start(f32[6,1,128,128]{3,2,1,0:T(8,128)} %get-tuple-element.181), channel_id=1, source_target_pairs={{0,1},{1,2},{2,3},{3,4},{4,5},{5,6},{6,7},{8,9},{9,10},{10,11},{11... | collective-permute-start | bytes 1179656 | tf_op jit(solution)/shard_map/ppermute | solution.py:34
  452.9 9.9 %collective-permute-start.59 = (f32[16,128,1]{1,0,2:T(8,128)S(1)}, f32[16,128,1]{1,0,2:T(8,128)S(1)}, u32[]{:S(2)}, u32[]{:S(2)}) collective-permute-start(f32[16,128,1]{1,0,2:T(8,128)S(1)} %copy.53), channel_id=1, source_target_pairs={{0,64},{8,72},{16,80},{24,88},{32,96},{40,104},{48,112},{56,120},{... | collective-permute-start | bytes 24584 | tf_op jit(solution)/shard_map/ppermute | solution.py:18
  (55 other events, 645.7 us)
Sparse Core Ops, SparseCore 0:
  63.9 76.0 all-reduce.2
where the time goes:
time: 512 us; the launch traced here: 508 us
  starting transfers between devices  272 us (53%)
  waiting for transfers between devices  170 us (33%)
  other arithmetic  26.6 us (5%)
  blocking collectives  17.9 us (3%)
  between operations  15.5 us (3%)
  local copies, waits for them, and re-layouts  6.29 us (1%)
    ppermute x36, starting transfers between devices, shifted(): return lax.ppermute(value, axis, pairs)  190 us
    psum x1, waiting for transfers between devices, body(): lax.psum((jnp.sum(flux_east, axis=0), jnp.sum(flux_north, axis=0), jnp.su...  73.9 us
    ppermute x36, waiting for transfers between devices, shifted(): return lax.ppermute(value, axis, pairs)  67 us
    ppermute x27, starting transfers between devices, from_behind(): return lax.ppermute(value, axis, pairs)  41.8 us
    ppermute x1, starting transfers between devices, with_halo(): after = lax.ppermute(leading, axis, down)  37.7 us
    ppermute x27, waiting for transfers between devices, from_behind(): return lax.ppermute(value, axis, pairs)  29.1 us
    all_gather x1, blocking collectives, prefix(): everything = lax.all_gather(value, axis)  17.9 us
  transfers between devices with their start and end apart: 66, of which 39 were waited for; matrix products, arithmetic and copies ran while one was open for 4% of the time, Pallas kernels for 0%

commit v1 on v0

v1 whole, which is shorter than its diff:
```python
import functools

import jax
import jax.numpy as jnp
from jax import lax
from jax.experimental import pallas as pl
from jax.experimental.pallas import tpu as pltpu
from jax.sharding import PartitionSpec as P

TROWS = 8
NSUB = 8
NTR = 6
ND = 8
CY = 128
CX = 128
RX = CY + 16

tau = 0.45
coupling = 1.0 / 16
tracer_time = 0.1

MESH = pl.DeviceIdType.MESH
F32 = jnp.float32


def roll(x, shift, axis):
    shift = shift % x.shape[axis]
    return x if shift == 0 else pltpu.roll(x, shift, axis)


def lanes(rows, width=CX):
    return lax.broadcasted_iota(jnp.int32, (rows, width), 1)


def rows_of(rows, width=CX):
    return lax.broadcasted_iota(jnp.int32, (rows, width), 0)


def between(x, low, high):
    return (x >= low) & (x < high)


def kernel(
    h_in, u_in, v_in, c_in, sea_in, uc_in, vc_in, wet_in, lev_in,
    c_out, s_out, e_out, n_out,
    h, u, v, c, sea, uc, vc, wet, lev,
    east_pack, west_pack, north_pack, south_pack,
    side_e, side_w, rim_n, rim_s,
    above, below,
    send_buf, recv_buf, total,
    face_e, face_n, u_ext, v_ext,
    surf, te, tn, tw, ae, be, ce, an, bn, cn,
    dep_e, dep_n, col_e, col_n,
    div_send, div_recv, new_c,
    loc_sem, halo_send, halo_recv, vert_send, vert_recv,
    rs_send, rs_recv, ag_send, ag_recv, div_ss, div_rs, out_sem,
):
    me = lax.axis_index("depth")
    tile = lax.axis_index("tiles")
    tx = tile // TROWS
    ty = tile % TROWS
    cols = 8

    def tile_at(dx, dy):
        return ((tx + dx + cols) % cols) * TROWS + (ty + dy + TROWS) % TROWS

    def member(which):
        return {"tiles": tile, "depth": which}

    def beside(dx, dy):
        return {"tiles": tile_at(dx, dy), "depth": me}

    around = [(1, 0), (-1, 0), (0, 1), (0, -1), (1, 1), (-1, 1), (1, -1), (-1, -1)]

    fetches = []
    for i, (src, dst) in enumerate([
        (h_in.at[:, 0], h), (u_in.at[:, 0], u), (v_in.at[:, 0], v), (sea_in.at[0], sea),
        (uc_in.at[0], uc), (vc_in.at[0], vc), (wet_in.at[0], wet), (lev_in.at[0], lev),
        (c_in.at[:, :, 0], c),
    ]):
        copy = pltpu.make_async_copy(src, dst, loc_sem.at[i])
        copy.start()
        fetches.append(copy)

    barrier = pltpu.get_barrier_semaphore()
    for dx, dy in around:
        pl.semaphore_signal(barrier, inc=1, device_id=beside(dx, dy), device_id_type=MESH)
    for k in range(1, ND):
        pl.semaphore_signal(barrier, inc=1, device_id=member((me + k) % ND), device_id_type=MESH)

    for copy in fetches:
        copy.wait()

    lane = lanes(CY)
    row = rows_of(CY)
    count = (wet[...] * lev[...]).astype(F32)
    fields = [h[0], h[1], u[0], u[1], v[0], v[1], count, sea[...], uc[...], vc[...]]
    to_east = jnp.zeros((CY, CX), F32)
    to_west = jnp.zeros((CY, CX), F32)
    for f, x in enumerate(fields):
        turned = roll(x, 8 * f, 1)
        start = (8 * f - 8) % CX
        to_west = jnp.where(between(lane, 8 * f, 8 * f + 8), turned, to_west)
        to_east = jnp.where(between(lane, start, start + 8), turned, to_east)
        south_pack[8 * f : 8 * f + 8] = x[0:8]
        north_pack[8 * f : 8 * f + 8] = x[CY - 8 : CY]
    to_east = jnp.where(between(lane, 72, 80), roll(uc[...], 88, 1), to_east)
    north_pack[80:88] = vc[CY - 16 : CY - 8]
    south_pack[80:88] = vc[0:8]
    for p in range(2 * NTR):
        plane = c[p // 2, p % 2]
        turned = roll(plane, 96 + p, 1)
        to_west = jnp.where(lane == 96 + p, turned, to_west)
        to_east = jnp.where(lane == 95 + p, turned, to_east)
        south_pack[88 + p : 89 + p] = plane[0:1]
        north_pack[88 + p : 89 + p] = plane[CY - 1 : CY]
    for p in range(2 * NTR, 16):
        south_pack[88 + p : 89 + p] = jnp.zeros((1, CX), F32)
        north_pack[88 + p : 89 + p] = jnp.zeros((1, CX), F32)
    east_pack[...] = to_east
    west_pack[...] = to_west

    first = (2 * me).astype(F32)
    count_e = jnp.minimum(count, jnp.where(lane == CX - 1, 0.0, roll(count, -1, 1)))
    count_n = jnp.minimum(count, jnp.where(row == CY - 1, 0.0, roll(count, -1, 0)))
    sums = [None] * 4
    for l in range(2):
        de = jnp.where(first + l < count_e, 0.5 * (h[l] + roll(h[l], -1, 1)), 0.0)
        dn = jnp.where(first + l < count_n, 0.5 * (h[l] + roll(h[l], -1, 0)), 0.0)
        for f, x in enumerate([de, dn, u[l] * de, v[l] * dn]):
            sums[f] = x if l == 0 else sums[f] + x
    for f in range(4):
        for p in range(ND):
            send_buf[p, 16 * f : 16 * f + 16] = sums[f][16 * p : 16 * p + 16]

    pl.semaphore_wait(barrier, len(around) + ND - 1)

    def halo(i, src, dst, dx, dy):
        return pltpu.make_async_remote_copy(
            src_ref=src, dst_ref=dst, send_sem=halo_send.at[i], recv_sem=halo_recv.at[i],
            device_id=beside(dx, dy), device_id_type=MESH,
        )

    halos = [
        halo(0, east_pack, side_w.at[0:CY], 1, 0),
        halo(1, west_pack, side_e.at[0:CY], -1, 0),
        halo(2, north_pack, rim_s, 0, 1),
        halo(3, south_pack, rim_n, 0, -1),
        halo(4, east_pack.at[CY - 8 : CY], side_w.at[CY + 8 : CY + 16], 1, 1),
        halo(5, west_pack.at[CY - 8 : CY], side_e.at[CY + 8 : CY + 16], -1, 1),
        halo(6, east_pack.at[0:8], side_w.at[CY : CY + 8], 1, -1),
        halo(7, west_pack.at[0:8], side_e.at[CY : CY + 8], -1, -1),
    ]
    for copy in halos:
        copy.start()

    def scatter(part, peer, slot):
        low, high = ((0, 64), (64, 88))[part]
        return pltpu.make_async_remote_copy(
            src_ref=send_buf.at[peer, low:high], dst_ref=recv_buf.at[slot, low:high],
            send_sem=rs_send.at[part, peer], recv_sem=rs_recv.at[part, slot],
            device_id=member(peer), device_id_type=MESH,
        )

    peers = [(me + k) % ND for k in range(1, ND)]
    for peer in peers:
        scatter(0, peer, me).start()

    up = pltpu.make_async_remote_copy(
        src_ref=c.at[:, 0], dst_ref=below, send_sem=vert_send.at[0], recv_sem=vert_recv.at[0],
        device_id=member((me + ND - 1) % ND), device_id_type=MESH,
    )
    down = pltpu.make_async_remote_copy(
        src_ref=c.at[:, 1], dst_ref=above, send_sem=vert_send.at[1], recv_sem=vert_recv.at[1],
        device_id=member((me + 1) % ND), device_id_type=MESH,
    )

    @pl.when(me > 0)
    def _():
        up.start()

    @pl.when(me == 0)
    def _():
        above[...] = jnp.zeros_like(above)

    @pl.when(me < ND - 1)
    def _():
        down.start()

    @pl.when(me == ND - 1)
    def _():
        below[...] = jnp.zeros_like(below)

    for copy in halos:
        copy.wait()

    lane_x = lanes(RX)
    row_x = rows_of(RX)
    has_n = ty < TROWS - 1
    has_s = ty > 0
    row_ok = (row_x < CY) | (between(row_x, CY, CY + 8) & has_n) | ((row_x >= CY + 8) & has_s)
    side_ok = row_ok & ((lane_x < 8) | (lane_x >= CX - 8))
    from_e = side_e[...]
    from_w = side_w[...]

    def extended(f, x):
        side = jnp.where(between(lane_x, 8 * f, 8 * f + 8), from_e, from_w)
        side = jnp.where(side_ok, roll(side, -8 * f, 1), 0.0)
        main = jnp.concatenate([x, rim_n[8 * f : 8 * f + 8], rim_s[8 * f : 8 * f + 8]], axis=0)
        main = jnp.where(row_ok, main, 0.0)
        return jnp.concatenate([main, side], axis=1)

    count_x = extended(6, count)
    min_e = jnp.minimum(count_x, roll(count_x, -1, 1))
    min_n = jnp.minimum(count_x, roll(count_x, -1, 0))
    sums = [None] * 4
    for l in range(2):
        h_x = extended(l, h[l])
        u_x = extended(2 + l, u[l])
        v_x = extended(4 + l, v[l])
        de = jnp.where(first + l < min_e, 0.5 * (h_x + roll(h_x, -1, 1)), 0.0)
        dn = jnp.where(first + l < min_n, 0.5 * (h_x + roll(h_x, -1, 0)), 0.0)
        face_e[l] = de
        face_n[l] = dn
        u_ext[l] = u_x
        v_ext[l] = v_x
        for f, x in enumerate([de, dn, u_x * de, v_x * dn]):
            sums[f] = x if l == 0 else sums[f] + x

    packed = jnp.zeros((RX, CX), F32)
    for f in range(4):
        packed = jnp.where(lane_x == 16 * f, roll(sums[f][:, :CX], 1 + 16 * f, 1), packed)
        packed = jnp.where(
            between(lane_x, 16 * f + 1, 16 * f + 16), roll(sums[f][:, CX:], 9 + 16 * f, 1), packed
        )
    half = RX // 2
    folded = jnp.where(lanes(half) < 64, packed[:half], roll(packed[half:], 64, 1))
    blocks = [folded[8 * i : 8 * i + 8] for i in range(9)]
    for f in range(4):
        blocks.append(roll(sums[f][:, :CX], 1, 0)[CY : CY + 8])
    for f in range(4):
        blocks.append(sums[f][CY + 8 : CY + 16, :CX])
    blocks += [jnp.zeros((8, CX), F32)] * (24 - len(blocks))
    for i, block in enumerate(blocks):
        low = 64 + 8 * (i % 3)
        send_buf[i // 3, low : low + 8] = block
    for peer in peers:
        scatter(1, peer, me).start()

    surf[...] = extended(7, sea[...])
    u_col = extended(8, uc[...])
    last = jnp.where(lane_x == CX - 9, roll(from_w, 40, 1), 0.0)
    te[...] = u_col + jnp.concatenate([jnp.zeros((RX, CX), F32), last], axis=1)
    tn[...] = extended(9, vc[...])
    wet_x = jnp.where(count_x > 0.0, 1.0, 0.0)
    tw[...] = tau * wet_x
    wet_e = wet_x * roll(wet_x, -1, 1)
    wet_n = wet_x * roll(wet_x, -1, 0)
    ae[...] = (1.0 - tau) * wet_e
    an[...] = (1.0 - tau) * wet_n

    for peer in peers:
        scatter(0, peer, peer).wait_recv()
        scatter(1, peer, peer).wait_recv()
    mine = send_buf[me]
    for k in range(1, ND):
        mine = mine + recv_buf[(me + k) % ND]
    total[me] = mine

    def gather(peer, slot):
        return pltpu.make_async_remote_copy(
            src_ref=total.at[slot], dst_ref=total.at[slot],
            send_sem=ag_send.at[peer], recv_sem=ag_recv.at[slot],
            device_id=member(peer), device_id_type=MESH,
        )

    for peer in peers:
        gather(peer, me).start()
    for peer in peers:
        gather(peer, peer).wait_recv()

    def block_of(i):
        low = 64 + 8 * (i % 3)
        return total[i // 3, low : low + 8]

    folded = jnp.concatenate([block_of(i) for i in range(9)], axis=0)
    packed = jnp.concatenate([folded, roll(folded, 64, 1)], axis=0)
    for f, ref in enumerate([dep_e, dep_n, col_e, col_n]):
        side = jnp.where((lane_x < 7) | (lane_x >= CX - 8), roll(packed, -(9 + 16 * f), 1), 0.0)
        north = block_of(9 + f)
        main = jnp.concatenate(
            [total[p, 16 * f : 16 * f + 16] for p in range(ND)]
            + [roll(north, -1, 0), block_of(13 + f)],
            axis=0,
        )
        main = jnp.where(row_x == CY - 1, jnp.broadcast_to(north[0:1], (RX, CX)), main)
        main = jnp.where(lane_x == CX - 1, roll(packed, CX - 1 - 16 * f, 1), main)
        ref[...] = jnp.concatenate([main, side], axis=1)
    be[...] = (tau * coupling) * wet_e * dep_e[...]
    bn[...] = (tau * coupling) * wet_n * dep_n[...]
    ce[...] = (tau * coupling) * wet_e * col_e[...]
    cn[...] = (tau * coupling) * wet_n * col_n[...]

    def substep(beyond):
        e = te[...]
        n = tn[...]
        south = roll(n, 1, 0)
        if beyond is not None:
            south = jnp.where(rows_of(RX, 2 * CX) == CY + 8, beyond, south)
        s = surf[...] - tw[...] * (e - roll(e, 1, 1) + n - south)
        surf[...] = s
        te[...] = ae[...] * e - be[...] * (roll(s, -1, 1) - s) + ce[...]
        tn[...] = an[...] * n - bn[...] * (roll(s, -1, 0) - s) + cn[...]

    beyond = jnp.concatenate([rim_s[87:88], jnp.zeros((1, CX), F32)], axis=1)
    substep(jnp.broadcast_to(beyond, (RX, 2 * CX)))

    def more(i, carry):
        substep(None)
        return carry

    lax.fori_loop(1, NSUB, more, 0)

    flat_out = [
        pltpu.make_async_copy(src.at[0:CY, 0:CX], dst.at[0], out_sem.at[i])
        for i, (src, dst) in enumerate([(surf, s_out), (te, e_out), (tn, n_out)])
    ]
    for copy in flat_out:
        copy.start()

    def parts_of(fe, fn):
        return fe[:, :CX], roll(fe, 1, 1)[:, :CX], fn[:CY], roll(fn, 1, 0)[:CY]

    shift_e = te[0:CY] - coupling * col_e[0:CY]
    shift_n = tn[:, 0:CX] - coupling * col_n[:, 0:CX]
    flows = []
    divs = []
    for l in range(2):
        fe, fw, fn, fs = parts_of(
            face_e[l, 0:CY] * (u_ext[l, 0:CY] + shift_e),
            face_n[l, :, 0:CX] * (v_ext[l, :, 0:CX] + shift_n),
        )
        flows.append((fe, fw, fn, fs))
        divs.append(fe - fw + fn - fs)
    here = divs[0] + divs[1]
    div_send[...] = here

    pair = me + 1 - 2 * (me % 2)
    upper = me < ND // 2
    outer = (me < 2) | (me >= ND - 2)
    near = jnp.where(upper, 2, ND - 4)

    def hand(i, slot, peer):
        return pltpu.make_async_remote_copy(
            src_ref=div_send, dst_ref=div_recv.at[slot], send_sem=div_ss.at[i], recv_sem=div_rs.at[slot],
            device_id=member(peer), device_id_type=MESH,
        )

    hand(0, 0, pair).start()

    @pl.when(outer)
    def _():
        hand(1, 1 + me % 2, near).start()
        hand(2, 1 + me % 2, near + 1).start()
        div_recv[1] = jnp.zeros((CY, CX), F32)
        div_recv[2] = jnp.zeros((CY, CX), F32)

    te_, tw_, tn_, ts_ = parts_of(
        col_e[0:CY] + dep_e[0:CY] * shift_e, col_n[:, 0:CX] + dep_n[:, 0:CX] * shift_n
    )
    whole = te_ - tw_ + tn_ - ts_

    gains = []
    for l in range(2):
        gain = jnp.where(first + l < count, tracer_time / h[l], 0.0)
        gains.append(gain)
        fe, fw, fn, fs = flows[l]
        a_e = -gain * jnp.minimum(fe, 0.0)
        a_w = gain * jnp.maximum(fw, 0.0)
        a_n = -gain * jnp.minimum(fn, 0.0)
        a_s = gain * jnp.maximum(fs, 0.0)
        a_c = 1.0 - gain * (
            jnp.maximum(fe, 0.0) - jnp.minimum(fw, 0.0) + jnp.maximum(fn, 0.0) - jnp.minimum(fs, 0.0)
        )
        for m in range(NTR):
            p = 2 * m + l
            x = c[m, l]
            x_e = jnp.where(lane == CX - 1, roll(side_e[0:CY], 31 - p, 1), roll(x, -1, 1))
            x_w = jnp.where(lane == 0, roll(side_w[0:CY], -(95 + p), 1), roll(x, 1, 1))
            x_n = jnp.where(
                row == CY - 1, jnp.broadcast_to(rim_n[88 + p : 89 + p], (CY, CX)), roll(x, -1, 0)
            )
            x_s = jnp.where(row == 0, jnp.broadcast_to(rim_s[88 + p : 89 + p], (CY, CX)), roll(x, 1, 0))
            new_c[m, l] = a_c * x + a_e * x_e + a_w * x_w + a_n * x_n + a_s * x_s

    hand(0, 0, pair).wait_recv()

    @pl.when(jnp.logical_not(outer))
    def _():
        hand(1, 1, pair).wait_recv()
        hand(2, 2, pair).wait_recv()

    partner = div_recv[0]
    far = div_recv[1] + div_recv[2]
    odd = me % 2 == 1
    deeper = jnp.where(
        upper,
        whole - here - far - jnp.where(odd, partner, 0.0),
        far + jnp.where(odd, 0.0, partner),
    )

    @pl.when(me < ND - 1)
    def _():
        up.wait_recv()

    @pl.when(me > 0)
    def _():
        down.wait_recv()

    bottom = -deeper
    middle = -(divs[1] + deeper)
    top = jnp.where(me == 0, 0.0, -(divs[0] + divs[1] + deeper))
    for l in range(2):
        low, high = (middle, top) if l == 0 else (bottom, middle)
        gain = gains[l]
        a_b = gain * jnp.maximum(low, 0.0)
        a_a = -gain * jnp.minimum(high, 0.0)
        a_c = gain * (jnp.minimum(low, 0.0) - jnp.maximum(high, 0.0))
        for m in range(NTR):
            under = c[m, 1] if l == 0 else below[m]
            over = above[m] if l == 0 else c[m, 0]
            new_c[m, l] = new_c[m, l] + a_c * c[m, l] + a_b * under + a_a * over
    store = pltpu.make_async_copy(new_c, c_out.at[:, :, 0], out_sem.at[3])
    store.start()

    for peer in peers:
        scatter(0, peer, me).wait_send()
        scatter(1, peer, me).wait_send()
        gather(peer, me).wait_send()
    hand(0, 0, pair).wait_send()

    @pl.when(outer)
    def _():
        hand(1, 1, near).wait_send()
        hand(2, 2, near).wait_send()

    @pl.when(me > 0)
    def _():
        up.wait_send()

    @pl.when(me < ND - 1)
    def _():
        down.wait_send()

    for copy in flat_out:
        copy.wait()
    store.wait()


def body(thickness, u_layer, v_layer, tracers, sea_level, u_column, v_column, wet_cells, levels):
    any_spec = pl.BlockSpec(memory_space=pl.ANY)
    plane = pltpu.VMEM((CY, CX), F32)
    layers = pltpu.VMEM((2, CY, CX), F32)
    wide = pltpu.VMEM((RX, 2 * CX), F32)
    wide2 = pltpu.VMEM((2, RX, 2 * CX), F32)
    whole_c = pltpu.VMEM((NTR, 2, CY, CX), F32)
    column_c = pltpu.VMEM((NTR, CY, CX), F32)
    side = pltpu.VMEM((RX, CX), F32)
    rim = pltpu.VMEM((104, CX), F32)
    pieces = pltpu.VMEM((ND, 88, CX), F32)
    flat = pltpu.VMEM((CY, CX), jnp.int32)
    dma = pltpu.SemaphoreType.DMA
    return pl.pallas_call(
        kernel,
        out_shape=(
            jax.ShapeDtypeStruct(tracers.shape, F32),
            jax.ShapeDtypeStruct(sea_level.shape, F32),
            jax.ShapeDtypeStruct(sea_level.shape, F32),
            jax.ShapeDtypeStruct(sea_level.shape, F32),
        ),
        in_specs=[any_spec] * 9,
        out_specs=(any_spec,) * 4,
        scratch_shapes=[
            layers, layers, layers, whole_c, plane, plane, plane, flat, flat,
            plane, plane, rim, rim,
            side, side, rim, rim,
            column_c, column_c,
            pieces, pieces, pieces,
            wide2, wide2, wide2, wide2,
            wide, wide, wide, wide, wide, wide, wide, wide, wide, wide,
            wide, wide, wide, wide,
            plane, pltpu.VMEM((3, CY, CX), F32), whole_c,
            dma((9,)), dma((8,)), dma((8,)), dma((2,)), dma((2,)),
            dma((2, ND)), dma((2, ND)), dma((ND,)), dma((ND,)), dma((3,)), dma((3,)), dma((4,)),
        ],
        compiler_params=pltpu.CompilerParams(
            collective_id=0, has_side_effects=True, vmem_limit_bytes=56 * 1024 * 1024
        ),
    )(thickness, u_layer, v_layer, tracers, sea_level, u_column, v_column, wet_cells, levels)


def solution(mesh):
    return jax.shard_map(
        body,
        mesh=mesh,
        in_specs=(
            P("depth", "tiles", None, None),
            P("depth", "tiles", None, None),
            P("depth", "tiles", None, None),
            P(None, "depth", "tiles", None, None),
            P("tiles", None, None),
            P("tiles", None, None),
            P("tiles", None, None),
            P("tiles", None, None),
            P("tiles", None, None),
        ),
        out_specs=(
            P(None, "depth", "tiles", None, None),
            P("tiles", None, None),
            P("tiles", None, None),
            P("tiles", None, None),
        ),
        check_vma=False,
    )
```

time: 512 us -> 45.5 us (0.09)
  the two profiles are of different devices: /device:TPU:1 before, /device:TPU:35 now
where the time goes in v1:
time: 45.5 us; the launch traced here: 45.2 us
  Pallas kernels  40.1 us (88%)
  local copies, waits for them, and re-layouts  4.45 us (10%)
  between operations  0.65 us (1%)
    pallas_call x1, Pallas kernels, body(): pl.pallas_call(kernel, out_shape=(jax.ShapeDtypeStruct(tracers.shape, F32...  40.1 us
    unnamed x10, local copies, waits for them, and re-layouts  4.45 us

profile of v1, /device:TPU:35, one launch (start us, length us, event | category | flops | bytes accessed | tf_op | source)
XLA Modules:
  0.0 45.2 jit_solution(6642874374139048314)
XLA Ops:
  0.6 40.1 %shard_map.120 = (f32[6,2,1,128,128]{4,3,2,1,0:T(8,128)}, f32[1,128,128]{2,1,0:T(8,128)}, f32[1,128,128]{2,1,0:T(8,128)}, f32[1,128,128]{2,1,0:T(8,128)}) custom-call(f32[2,1,128,128]{3,2,1,0:T(8,128)} %h_in.1, f32[2,1,128,128]{3,2,1,0:T(8,128)} %u_in.1, f32[2,1,128,128]{3,2,1,0:T(8,128)} %v_in.1, f32[6,2,1,128,128]{4,3,2,1,0:T(8,128)} %c_in.1, ...), custom_call_target="tpu_custom_call" | custom-call | tf_op jit(solution)/shard_map/pallas_call | solution.py:473
  40.8 0.0 copy-start.2
  40.8 2.1 %copy.17 = f32[6,2,1,128,128]{4,3,2,1,0:T(8,128)} copy(f32[6,2,1,128,128]{4,3,2,1,0:T(8,128)} %get-tuple-element.8) | data formatting | bytes 1572864
  42.9 0.0 copy-done.2
  42.9 0.0 copy-start.1
  42.9 0.6 %copy.18 = f32[1,128,128]{2,1,0:T(8,128)} copy(f32[1,128,128]{2,1,0:T(8,128)S(1)} %copy-done.2) | data formatting | bytes 131072
  43.5 0.2 copy-done.1
  43.7 0.0 copy-start
  43.7 0.6 %copy.19 = f32[1,128,128]{2,1,0:T(8,128)} copy(f32[1,128,128]{2,1,0:T(8,128)S(1)} %copy-done.1) | data formatting | bytes 131072
  44.4 0.2 copy-done
  44.6 0.6 %copy.20 = f32[1,128,128]{2,1,0:T(8,128)} copy(f32[1,128,128]{2,1,0:T(8,128)S(1)} %copy-done) | data formatting | bytes 131072
Async XLA Ops:
  40.8 2.1 %copy-start.2 = (f32[1,128,128]{2,1,0:T(8,128)S(1)}, f32[1,128,128]{2,1,0:T(8,128)}, u32[]{:S(2)}) copy-start(f32[1,128,128]{2,1,0:T(8,128)} %get-tuple-element.9) | copy-start | bytes 196612
  42.9 0.9 %copy-start.1 = (f32[1,128,128]{2,1,0:T(8,128)S(1)}, f32[1,128,128]{2,1,0:T(8,128)}, u32[]{:S(2)}) copy-start(f32[1,128,128]{2,1,0:T(8,128)} %get-tuple-element.10) | copy-start | bytes 196612
  43.7 0.9 %copy-start = (f32[1,128,128]{2,1,0:T(8,128)S(1)}, f32[1,128,128]{2,1,0:T(8,128)}, u32[]{:S(2)}) copy-start(f32[1,128,128]{2,1,0:T(8,128)} %get-tuple-element.11) | copy-start | bytes 196612

commit v2 on v0

v2 whole, which is shorter than its diff:
```python
import functools

import jax
import jax.numpy as jnp
from jax import lax
from jax.experimental import pallas as pl
from jax.experimental.pallas import tpu as pltpu
from jax.sharding import PartitionSpec as P

TROWS = 8
NSUB = 8
NTR = 6
ND = 8
NE = 4
EB = 5
CY = 128
CX = 128
RX = CY + 32
OWN = 16
END = OWN + CY
LOW = OWN - 8
HIGH = END + 8

tau = 0.45
coupling = 1.0 / 16
tracer_time = 0.1

MESH = pl.DeviceIdType.MESH
F32 = jnp.float32


def roll(x, shift, axis):
    shift = shift % x.shape[axis]
    return x if shift == 0 else pltpu.roll(x, shift, axis)


def lanes(rows, width=CX):
    return lax.broadcasted_iota(jnp.int32, (rows, width), 1)


def rows_of(rows, width=CX):
    return lax.broadcasted_iota(jnp.int32, (rows, width), 0)


def between(x, low, high):
    return (x >= low) & (x < high)


def kernel(
    h_in, u_in, v_in, c_in, sea_in, uc_in, vc_in, wet_in, lev_in,
    part, s_out, e_out, n_out, c, below, above, lift,
    x, state, wet, lev,
    side_pack, side_in, corner_pack, corner_in, sizes,
    edge_c,
    main_send, pair_in, chip_sum, main_in, main_all,
    edge_send, edge_in, edge_all,
    face_e, face_n, local, total,
    tw, ae, an, be, bn, ce, cn,
    outer_send, outer_pair, outer_sum, outer_in, outer_div,
    flow_n, flow_t, prod_n, coef, div_1, whole_div, pair_send, pair_div,
    loc_sem, sent, sent_late, edge_sent, outer_sent, up_sent, down_sent,
    halo_got, pair_got, rs_got, ag_got, forward_got, edge_got, edge_all_got, half_got, outer_got,
    up_got, down_got, div_got,
):
    me = lax.axis_index("depth")
    tile = lax.axis_index("tiles")
    tx = tile // TROWS
    ty = tile % TROWS
    chip = me // 2
    core = me % 2
    other = 1 - core
    partner = 2 * chip + other
    upper = me < ND // 2
    outer = (me < 2) | (me >= ND - 2)
    cols = 8

    def tile_at(dx, dy):
        return ((tx + dx + cols) % cols) * TROWS + (ty + dy + TROWS) % TROWS

    def member(which):
        return {"tiles": tile, "depth": which}

    def beside(dx, dy):
        return {"tiles": tile_at(dx, dy), "depth": me}

    def remote(source, target, send, recv, where):
        return pltpu.make_async_remote_copy(
            src_ref=source, dst_ref=target, send_sem=send, recv_sem=recv,
            device_id=where, device_id_type=MESH,
        )

    around = [(1, 0), (-1, 0), (0, 1), (0, -1), (1, 1), (-1, 1), (1, -1), (-1, -1)]
    rows_own = slice(OWN, END)

    def got(sem, rows):
        remote(sizes.at[0:rows], sizes.at[0:rows], sem, sem, member(partner)).wait_recv()

    def left(sem, rows):
        remote(sizes.at[0:rows], sizes.at[0:rows], sem, sem, member(partner)).wait_send()

    for source, target in [
        (h_in.at[:, 0], x.at[0:2, 0, rows_own]), (wet_in.at[0], wet), (lev_in.at[0], lev),
        (u_in.at[:, 0], x.at[2:4, 0, rows_own]), (v_in.at[:, 0], x.at[4:6, 0, rows_own]),
        (sea_in.at[0], state.at[0, 0, rows_own]), (uc_in.at[0], state.at[1, 0, rows_own]),
        (vc_in.at[0], state.at[2, 0, rows_own]),
    ]:
        pltpu.make_async_copy(source, target, loc_sem.at[0]).start()

    barrier = pltpu.get_barrier_semaphore()
    for dx, dy in around:
        pl.semaphore_signal(barrier, inc=1, device_id=beside(dx, dy), device_id_type=MESH)
    peers = [(me + k) % ND for k in range(1, ND)]
    for peer in peers:
        pl.semaphore_signal(barrier, inc=1, device_id=member(peer), device_id_type=MESH)
    fetch_c = pltpu.make_async_copy(c_in.at[:, :, 0], c.at[:, :, 8 : CY + 8], loc_sem.at[1])
    fetch_c.start()

    fetched = 11 * CY
    pltpu.make_async_copy(sizes.at[0:fetched], sizes.at[0:fetched], loc_sem.at[0]).wait()

    lane8 = lanes(8)
    x[6, 0, rows_own] = (wet[...] * lev[...]).astype(F32)

    def pack_sides(phase, fields, extra=None):
        for i in range(8):
            east = west = jnp.zeros((8, CX), F32)
            for j in range(2):
                low = OWN + 64 * j + 8 * i
                for f, ref in enumerate(fields):
                    turned = roll(ref[low : low + 8], 8 * f + 8 + 64 * j, 1)
                    start = 64 * j + 8 * f
                    west = jnp.where(between(lane8, start + 8, start + 16), turned, west)
                    east = jnp.where(between(lane8, start, start + 8), turned, east)
                if extra is not None:
                    east, west = extra(64 * j + 8 * i, 64 * j, east, west)
            side_pack[phase, 0, 8 * i : 8 * i + 8] = east
            side_pack[phase, 1, 8 * i : 8 * i + 8] = west

    early = [x.at[f, 0] for f in range(7)]
    late = [state.at[f, 0] for f in range(3)]
    pack_sides(0, early)

    for j, low in enumerate((OWN, END - 8)):
        east = west = jnp.zeros((8, CX), F32)
        for f, ref in enumerate(early + late):
            turned = roll(ref[low : low + 8], 8 * f + 8, 1)
            west = jnp.where(between(lane8, 8 * f + 8, 8 * f + 16), turned, west)
            east = jnp.where(between(lane8, 8 * f, 8 * f + 8), turned, east)
        corner_pack[0, j] = east
        corner_pack[1, j] = west

    pl.semaphore_wait(barrier, len(around) + ND - 1)

    def halo(phase, source, target, dx, dy):
        sem = sent if phase == 0 else sent_late
        remote(source, target, sem, halo_got.at[phase], beside(dx, dy)).start()

    halo(0, side_pack.at[0, 0], side_in.at[0, 0], 1, 0)
    halo(0, side_pack.at[0, 1], side_in.at[0, 1], -1, 0)
    halo(0, corner_pack.at[0, 1], corner_in.at[0], 1, 1)
    halo(0, corner_pack.at[1, 1], corner_in.at[1], -1, 1)
    halo(0, corner_pack.at[0, 0], corner_in.at[2], 1, -1)
    halo(0, corner_pack.at[1, 0], corner_in.at[3], -1, -1)
    halo(0, x.at[:, 0, END - 8 : END], x.at[:, 0, LOW:OWN], 0, 1)
    halo(0, x.at[:, 0, OWN : OWN + 8], x.at[:, 0, END:HIGH], 0, -1)

    first = (2 * me).astype(F32)
    lane16 = lanes(16)
    row16 = rows_of(16)

    def next_row(ref, p):
        low = OWN + 16 * p
        if p < ND - 1:
            return ref[low + 1 : low + 17]
        return jnp.where(row16 == 15, 0.0, roll(ref[low : low + 16], -1, 0))

    for p in range(ND):
        low = OWN + 16 * p
        here = slice(low, low + 16)
        count = x[6, 0, here]
        count_e = jnp.minimum(count, jnp.where(lane16 == CX - 1, 0.0, roll(count, -1, 1)))
        count_n = jnp.minimum(count, next_row(x.at[6, 0], p))
        sums = [0.0] * 4
        for l in range(2):
            thick = x[l, 0, here]
            de = jnp.where(first + l < count_e, 0.5 * (thick + roll(thick, -1, 1)), 0.0)
            dn = jnp.where(first + l < count_n, 0.5 * (thick + next_row(x.at[l, 0], p)), 0.0)
            new = [de, dn, x[2 + l, 0, here] * de, x[4 + l, 0, here] * dn]
            sums = [a + b for a, b in zip(sums, new)]
        for f in range(4):
            main_send[p // 2, p % 2, 16 * f : 16 * f + 16] = sums[f]
    remote(main_send.at[:, other], pair_in, sent, pair_got, member(partner)).start()

    fetch_c.wait()
    rows_c = slice(8, CY + 8)

    def send_tracers(i):
        part = slice(2 * i, 2 * i + 2)

        @pl.when(me > 0)
        def _():
            remote(
                c.at[part, 0, rows_c], below.at[part], up_sent, up_got, member((me + ND - 1) % ND)
            ).start()

        @pl.when(me < ND - 1)
        def _():
            remote(
                c.at[part, 1, rows_c], above.at[part], down_sent, down_got, member((me + 1) % ND)
            ).start()

    send_tracers(0)

    def pack_more(low, shift, east, west):
        old = state[1, 0, OWN + low : OWN + low + 8]
        east = jnp.where(between(lane8, shift + 24, shift + 32), roll(old, 40 + shift, 1), east)
        for p in range(2 * NTR):
            plane = c[p // 2, p % 2, 8 + low : 16 + low]
            west = jnp.where(lane8 == shift + 48 + p, roll(plane, shift + 48 + p, 1), west)
            east = jnp.where(lane8 == shift + 49 + p, roll(plane, shift + 50 + p, 1), east)
        return east, west

    pack_sides(1, late, pack_more)

    got(pair_got, 256)
    chips = [(chip + k) % 4 for k in range(1, 4)]
    for q in range(4):
        chip_sum[q] = main_send[q, core] + pair_in[q]
    for q in chips:
        remote(chip_sum.at[q], main_in.at[chip], sent, rs_got, member(2 * q + core)).start()
    send_tracers(1)
    halo(1, side_pack.at[1, 0], side_in.at[1, 0], 1, 0)
    halo(1, side_pack.at[1, 1], side_in.at[1, 1], -1, 0)
    halo(1, state.at[:, 0, END - 16 : END], state.at[:, 0, 0:OWN], 0, 1)
    halo(1, state.at[:, 0, OWN : OWN + 8], state.at[:, 0, END:HIGH], 0, -1)
    halo(1, c.at[:, :, CY : CY + 8], c.at[:, :, 0:8], 0, 1)
    halo(1, c.at[:, :, 8:16], c.at[:, :, CY + 8 : CY + 16], 0, -1)

    @pl.when(me == 0)
    def _():
        above[...] = jnp.zeros_like(above)

    @pl.when(me == ND - 1)
    def _():
        below[...] = jnp.zeros_like(below)

    for ref in (x, state):
        for k in range(2):
            ref[:, k, HIGH:RX] = jnp.zeros((ref.shape[0], RX - HIGH, CX), F32)
    state[2, 1, 0:LOW] = jnp.zeros((LOW, CX), F32)

    has_n = ty < TROWS - 1
    has_s = ty > 0

    def unpack_sides(phase, fields, extra=None):
        side = (lane8 < 8) | (lane8 >= CX - 8)
        for i in range(-1, 17):
            if i < 0:
                west, east, shift, ok = corner_in[0], corner_in[1], 56 * phase, side & has_s
            elif i == 16:
                west, east, shift, ok = corner_in[2], corner_in[3], 56 * phase, side & has_n
            else:
                j = 8 * (i % 8)
                west, east = side_in[phase, 0, j : j + 8], side_in[phase, 1, j : j + 8]
                shift, ok = 64 * (i // 8), side
            low = OWN + 8 * i
            for f, ref in enumerate(fields):
                start = shift + 8 * f + 8
                value = roll(jnp.where(between(lane8, start, start + 8), east, west), -start, 1)
                value = jnp.where(ok, value, 0.0)
                if extra is not None and f == 1 and 0 <= i < 16:
                    value = jnp.where(lane8 == CX - 9, roll(west, 88 - shift, 1), value)
                ref[low : low + 8] = value
            if extra is not None and 0 <= i < 16:
                extra(8 * i, shift, west, east)

    got(halo_got.at[0], 272)
    unpack_sides(0, [x.at[f, 1] for f in range(7)])

    @pl.when(jnp.logical_not(has_s))
    def _():
        x[:, 0, LOW:OWN] = jnp.zeros((7, 8, CX), F32)

    @pl.when(jnp.logical_not(has_n))
    def _():
        x[:, 0, END:HIGH] = jnp.zeros((7, 8, CX), F32)

    def shifted(pair, steps):
        lane = lanes(pair[0].shape[0])
        edge = lane == (0 if steps > 0 else CX - 1)
        main, side = (roll(value, steps, 1) for value in pair)
        return jnp.where(edge, side, main), jnp.where(edge, main, side)

    def both(ref, low, size):
        return ref[0, low : low + size], ref[1, low : low + size]

    step = 24
    for low in range(LOW, HIGH, step):
        here = slice(low, low + step)
        count = both(x.at[6], low, step)
        count_e = shifted(count, -1)
        count_n = both(x.at[6], low + 1, step)
        thick = [both(x.at[l], low, step) for l in range(2)]
        thick_e = [shifted(thick[l], -1) for l in range(2)]
        for k in range(2):
            min_e = jnp.minimum(count[k], count_e[k])
            min_n = jnp.minimum(count[k], count_n[k])
            sums = [0.0] * 4
            for l in range(2):
                north = x[l, k, low + 1 : low + 1 + step]
                de = jnp.where(first + l < min_e, 0.5 * (thick[l][k] + thick_e[l][k]), 0.0)
                dn = jnp.where(first + l < min_n, 0.5 * (thick[l][k] + north), 0.0)
                face_e[l, k, here] = de
                face_n[l, k, here] = dn
                new = [de, dn, x[2 + l, k, here] * de, x[4 + l, k, here] * dn]
                sums = [a + b for a, b in zip(sums, new)]
            for f in range(4):
                local[f, k, here] = sums[f]

    def put_block(i, block):
        edge_send[i // EB, 8 * (i % EB) : 8 * (i % EB) + 8] = block

    for i in range(9):
        block = jnp.zeros((8, CX), F32)
        for j in range(2):
            low = LOW + 72 * j + 8 * i
            for f in range(4):
                start = 64 * j + 16 * f
                block = jnp.where(
                    lane8 == start, roll(local[f, 0, low : low + 8], start + 1, 1), block
                )
                block = jnp.where(
                    between(lane8, start + 1, start + 16),
                    roll(local[f, 1, low : low + 8], start + 9, 1),
                    block,
                )
        put_block(i, block)
    for f in range(4):
        put_block(9 + f, local[f, 0, END - 1 : END + 7])
        put_block(13 + f, local[f, 0, LOW:OWN])
    for i in range(17, NE * EB):
        put_block(i, jnp.zeros((8, CX), F32))

    owner = core == 0

    @pl.when(owner)
    def _():
        for q in chips:
            remote(edge_send.at[q], edge_in.at[me], edge_sent, edge_got, member(2 * q)).start()

    @pl.when(jnp.logical_not(owner))
    def _():
        for q in chips + [chip]:
            remote(edge_send.at[q], edge_in.at[me], edge_sent, edge_got, member(2 * q)).start()

    @pl.when(outer)
    def _():
        for i in range(4):
            low = OWN + 32 * i
            here = slice(low, low + 32)
            flux = both(local.at[2], low, 32)
            value = flux[0] - shifted(flux, 1)[0] + local[3, 0, here] - local[3, 0, low - 1 : low + 31]
            outer_send[i // 2, 32 * (i % 2) : 32 * (i % 2) + 32] = value
        for j in range(2):
            low = OWN + 64 * j
            outer_send[j, 64:128] = local[0, 0, low : low + 64]
            outer_send[j, 128:200] = local[1, 0, low - 8 : low + 64]
            block = jnp.zeros((8, CX), F32)
            for r in range(8):
                turned = roll(local[0, 1, low + 8 * r : low + 8 * r + 8], r + 1, 1)
                block = jnp.where(lane8 == r, turned, block)
            outer_send[j, 200:208] = block
        remote(outer_send.at[other], outer_pair, outer_sent, half_got, member(partner)).start()

    got(rs_got, 192)
    mine = chip_sum[chip]
    for q in chips:
        mine = mine + main_in[q]
    main_all[chip, core] = mine
    piece = main_all.at[chip, core]
    for q in chips:
        remote(piece, piece, sent, ag_got, member(2 * q + core)).start()

    @pl.when(owner)
    def _():
        got(edge_got, 7 * 8 * EB)
        edge = edge_send[chip]
        for peer in peers:
            edge = edge + edge_in[peer]
        edge_all[chip] = edge
        for peer in peers:
            remote(edge_all.at[chip], edge_all.at[chip], edge_sent, edge_all_got, member(peer)).start()

    @pl.when(outer)
    def _():
        got(half_got, 208)
        outer_sum[...] = outer_send[core] + outer_pair[...]
        middle_chip = jnp.where(upper, 2, ND - 4)
        remote(outer_sum, outer_in, outer_sent, outer_got, member(middle_chip + core)).start()

    send_tracers(2)

    got(halo_got.at[1], 392)

    def put_tracers(low, shift, west, east):
        for p in range(2 * NTR):
            value = jnp.where(lane8 <= shift + 48 + p, east, west)
            edge_c[p // 2, p % 2, low : low + 8] = roll(value, 79 - shift - p, 1)

    unpack_sides(1, [state.at[f, 1] for f in range(3)], put_tracers)
    left(sent_late, 392)

    @pl.when(jnp.logical_not(has_s))
    def _():
        state[:, 0, LOW:OWN] = jnp.zeros((3, 8, CX), F32)

    @pl.when(jnp.logical_not(has_n))
    def _():
        state[:, 0, END:HIGH] = jnp.zeros((3, 8, CX), F32)

    for low in range(LOW, HIGH, step):
        here = slice(low, low + step)
        is_wet = [jnp.where(value > 0.0, 1.0, 0.0) for value in both(x.at[6], low, step)]
        wet_e = shifted(is_wet, -1)
        wet_n = [jnp.where(value > 0.0, 1.0, 0.0) for value in both(x.at[6], low + 1, step)]
        for k in range(2):
            tw[k, here] = tau * is_wet[k]
            ae[k, here] = (1.0 - tau) * (is_wet[k] * wet_e[k])
            an[k, here] = (1.0 - tau) * (is_wet[k] * wet_n[k])
            be[k, here] = (tau * coupling) * (is_wet[k] * wet_e[k])
            bn[k, here] = (tau * coupling) * (is_wet[k] * wet_n[k])

    got(ag_got, 192)
    half = main_all.at[:, core]
    remote(half, half, sent, forward_got, member(partner)).start()

    @pl.when(owner)
    def _():
        got(edge_all_got, 3 * 8 * EB)

    @pl.when(jnp.logical_not(owner))
    def _():
        got(edge_all_got, 4 * 8 * EB)

    got(forward_got, 256)

    def block_of(i):
        return edge_all[i // EB, 8 * (i % EB) : 8 * (i % EB) + 8]

    for f in range(4):
        for p in range(ND):
            low = OWN + 16 * p
            total[f, 0, low : low + 16] = main_all[p // 2, p % 2, 16 * f : 16 * f + 16]
        total[f, 0, END - 1 : END + 7] = block_of(9 + f)
        total[f, 0, HIGH - 1 : HIGH] = jnp.zeros((1, CX), F32)
        total[f, 0, LOW:OWN] = block_of(13 + f)
    rim = (lane8 < 7) | (lane8 >= CX - 8)
    for i in range(18):
        block = block_of(i % 9)
        shift = 64 * (i // 9)
        here = slice(LOW + 8 * i, LOW + 8 * i + 8)
        for f in range(4):
            edge = jnp.where(lane8 == CX - 1, roll(block, CX - 1 - 16 * f - shift, 1), total[f, 0, here])
            side = jnp.where(rim, roll(block, -(9 + 16 * f + shift), 1), 0.0)
            total[f, 0, here] = edge
            total[f, 1, here] = side
            for k, value in enumerate((edge, side)):
                if f == 2:
                    ce[k, here] = be[k, here] * value
                if f == 3:
                    cn[k, here] = bn[k, here] * value
        for k in range(2):
            be[k, here] = be[k, here] * total[0, k, here]
            bn[k, here] = bn[k, here] * total[1, k, here]

    def substep(i, carry):
        def rise(low):
            here = slice(low, low + step)
            east = both(state.at[1], low, step)
            west = shifted(east, 1)
            north = both(state.at[2], low, step)
            south = both(state.at[2], low - 1, step)
            level = []
            for k in range(2):
                value = state[0, k, here] - tw[k, here] * (east[k] - west[k] + north[k] - south[k])
                state[0, k, here] = value
                level.append(value)
            return level, east, north

        def move(low, level, east, north):
            here = slice(low, low + step)
            level_e = shifted(level, -1)
            level_n = both(state.at[0], low + 1, step)
            for k in range(2):
                state[1, k, here] = ae[k, here] * east[k] - be[k, here] * (level_e[k] - level[k]) + ce[k, here]
                state[2, k, here] = an[k, here] * north[k] - bn[k, here] * (level_n[k] - level[k]) + cn[k, here]

        held = rise(LOW)
        for low in range(LOW, HIGH, step):
            coming = rise(low + step) if low + step < HIGH else None
            move(low, *held)
            held = coming
        return carry

    lax.fori_loop(0, NSUB, substep, 0)

    flow_rows = [(OWN - 8, 8)] + [(OWN + 32 * i, 32) for i in range(4)]
    for low, size in flow_rows:
        here = slice(low, low + size)
        shift_n = state[2, 0, here] - coupling * total[3, 0, here]
        for l in range(2):
            flow_n[l, here] = face_n[l, 0, here] * (x[4 + l, 0, here] + shift_n)
        flow_t[here] = total[3, 0, here] + total[1, 0, here] * shift_n
        prod_n[here] = shift_n

    for i in range(4):
        low = OWN + 32 * i
        here = slice(low, low + 32)
        mine = slice(32 * i, 32 * i + 32)
        shift_e = [state[1, k, here] - coupling * total[2, k, here] for k in range(2)]
        flow = [total[2, k, here] + total[0, k, here] * shift_e[k] for k in range(2)]
        whole_div[mine] = flow[0] - shifted(flow, 1)[0] + flow_t[here] - flow_t[low - 1 : low + 31]
        count = x[6, 0, here]
        divs = []
        for l in range(2):
            flow = [face_e[l, k, here] * (x[2 + l, k, here] + shift_e[k]) for k in range(2)]
            fe = flow[0]
            fw = shifted(flow, 1)[0]
            fn = flow_n[l, here]
            fs = flow_n[l, low - 1 : low + 31]
            divs.append(fe - fw + fn - fs)
            gain = jnp.where(first + l < count, tracer_time / x[l, 0, here], 0.0)
            plus_e, minus_w = jnp.maximum(fe, 0.0), jnp.minimum(fw, 0.0)
            plus_n, minus_s = jnp.maximum(fn, 0.0), jnp.minimum(fs, 0.0)
            coef[l, 0, mine] = gain * (plus_e - fe)
            coef[l, 1, mine] = gain * (fw - minus_w)
            coef[l, 2, mine] = gain * (plus_n - fn)
            coef[l, 3, mine] = gain * (fs - minus_s)
            coef[l, 4, mine] = 1.0 - gain * (plus_e - minus_w + plus_n - minus_s)
            coef[l, 5, mine] = gain
        div_1[mine] = divs[1]
        pair_send[mine] = divs[0] + divs[1]

    @pl.when(jnp.logical_not(outer))
    def _():
        got(outer_got, 208)
        base = pl.multiple_of(OWN + 64 * core, 8)
        here = pl.ds(base, 64)
        shift_e = [state[1, k, here] - coupling * total[2, k, here] for k in range(2)]
        flow = outer_in[64:128] * shift_e[0]
        block = outer_in[200:208]
        column = jnp.concatenate([roll(block, -r, 1) for r in range(8)], axis=0)
        west = jnp.where(lanes(64) == 0, column * roll(shift_e[1], 1, 1), roll(flow, 1, 1))
        flow_t[0:72] = outer_in[128:200] * prod_n[pl.ds(pl.multiple_of(base - 8, 8), 72)]
        value = outer_in[0:64] + flow - west + flow_t[8:72] - flow_t[7:71]
        outer_div[core] = value
        pair_send[CY : CY + 64] = value

    remote(pair_send, pair_div, sent, div_got, member(partner)).start()

    s_out[0] = state[0, 0, rows_own]
    e_out[0] = state[1, 0, rows_own]
    n_out[0] = state[2, 0, rows_own]

    lane32 = lanes(32)
    for l in range(2):
        for i in range(4):
            mine = slice(32 * i, 32 * i + 32)
            low = 8 + 32 * i
            a_e, a_w, a_n, a_s, a_c = (coef[l, j, mine] for j in range(5))
            for m in range(NTR):
                value = c[m, l, low : low + 32]
                edge = edge_c[m, l, mine]
                value_e = jnp.where(lane32 == CX - 1, edge, roll(value, -1, 1))
                value_w = jnp.where(lane32 == 0, edge, roll(value, 1, 1))
                part[m, l, mine] = (
                    a_c * value
                    + a_e * value_e
                    + a_w * value_w
                    + a_n * c[m, l, low + 1 : low + 33]
                    + a_s * c[m, l, low - 1 : low + 31]
                )

    left(sent, 1360)

    @pl.when(owner)
    def _():
        left(edge_sent, 10 * 8 * EB)

    @pl.when(jnp.logical_not(owner))
    def _():
        left(edge_sent, 4 * 8 * EB)

    @pl.when(outer)
    def _():
        left(outer_sent, 416)

    got(div_got, 192)

    @pl.when(jnp.logical_not(outer))
    def _():
        outer_div[other] = pair_div[CY : CY + 64]

    @pl.when(outer)
    def _():
        outer_div[...] = jnp.zeros_like(outer_div)

    odd = core == 1
    for i in range(4):
        mine = slice(32 * i, 32 * i + 32)
        beyond = outer_div[i // 2, 32 * (i % 2) : 32 * (i % 2) + 32]
        near = pair_div[mine]
        here = pair_send[mine]
        deeper = jnp.where(
            upper,
            whole_div[mine] - here - beyond - jnp.where(odd, near, 0.0),
            beyond + jnp.where(odd, 0.0, near),
        )
        bottom = -deeper
        middle = -(div_1[mine] + deeper)
        top = jnp.where(me == 0, 0.0, -(here + deeper))
        for l in range(2):
            under_flow, over_flow = (middle, top) if l == 0 else (bottom, middle)
            gain = coef[l, 5, mine]
            lift[l, 0, mine] = gain * (jnp.minimum(under_flow, 0.0) - jnp.maximum(over_flow, 0.0))
            lift[l, 1, mine] = gain * jnp.maximum(under_flow, 0.0)
            lift[l, 2, mine] = -gain * jnp.minimum(over_flow, 0.0)

    @pl.when(me < ND - 1)
    def _():
        got(up_got, NTR * CY)
        left(down_sent, NTR * CY)

    @pl.when(me > 0)
    def _():
        got(down_got, NTR * CY)
        left(up_sent, NTR * CY)


def store(part, s_ref, e_ref, n_ref, c, below, above, lift, c_out, s_out, e_out, n_out, new_c, sem):
    copies = [
        pltpu.make_async_copy(source, target, sem.at[NTR + i])
        for i, (source, target) in enumerate([(s_ref, s_out), (e_ref, e_out), (n_ref, n_out)])
    ]
    for copy in copies:
        copy.start()
    for pair in range(0, NTR, 2):
        for l in range(2):
            for i in range(4):
                mine = slice(32 * i, 32 * i + 32)
                low = 8 + 32 * i
                a_c, a_b, a_a = (lift[l, j, mine] for j in range(3))
                for m in (pair, pair + 1):
                    under = c[m, 1, low : low + 32] if l == 0 else below[m, mine]
                    over = above[m, mine] if l == 0 else c[m, 0, low : low + 32]
                    new_c[m, l, mine] = (
                        part[m, l, mine] + a_c * c[m, l, low : low + 32] + a_b * under + a_a * over
                    )
        for m in (pair, pair + 1):
            copy = pltpu.make_async_copy(new_c.at[m], c_out.at[m, :, 0], sem.at[m])
            copy.start()
            copies.append(copy)
    for copy in copies:
        copy.wait()


def body(thickness, u_layer, v_layer, tracers, sea_level, u_column, v_column, wet_cells, levels):
    any_spec = pl.BlockSpec(memory_space=pl.ANY)
    near_spec = pl.BlockSpec(memory_space=pltpu.VMEM)

    def vmem(*shape):
        return pltpu.VMEM(shape, F32)

    plane = vmem(CY, CX)
    wide = vmem(2, RX, CX)
    wide2 = vmem(2, 2, RX, CX)
    column_c = vmem(NTR, CY, CX)
    flat = pltpu.VMEM((CY, CX), jnp.int32)
    quarter = vmem(4, 64, CX)
    halves = vmem(4, 2, 64, CX)
    edges = vmem(NE, 8 * EB, CX)
    dma = pltpu.SemaphoreType.DMA
    shapes = [tracers.shape] + [sea_level.shape] * 3
    results = pl.pallas_call(
        kernel,
        out_shape=(
            vmem(NTR, 2, CY, CX), *(pltpu.VMEM(shape, F32) for shape in shapes[1:]),
            vmem(NTR, 2, CY + 16, CX), column_c, column_c, vmem(2, 3, CY, CX),
        ),
        in_specs=[pl.BlockSpec(memory_space=pltpu.HBM)] * 9,
        out_specs=(near_spec,) * 8,
        scratch_shapes=[
            vmem(7, 2, RX, CX), vmem(3, 2, RX, CX), flat, flat,
            vmem(2, 2, 64, CX), vmem(2, 2, 64, CX), vmem(2, 2, 8, CX), vmem(4, 8, CX), vmem(11 * CY, CX),
            vmem(NTR, 2, CY, CX),
            halves, quarter, quarter, quarter, halves,
            edges, vmem(ND, 8 * EB, CX), edges,
            wide2, wide2, vmem(4, 2, RX, CX), vmem(4, 2, RX, CX),
            wide, wide, wide, wide, wide, wide, wide,
            vmem(2, 208, CX), vmem(208, CX), vmem(208, CX), vmem(208, CX), vmem(2, 64, CX),
            vmem(2, RX, CX), vmem(RX, CX), vmem(RX, CX), vmem(2, 6, CY, CX),
            plane, plane, vmem(CY + 64, CX), vmem(CY + 64, CX),
            dma((2,)), dma, dma, dma, dma, dma, dma,
            dma((2,)), dma, dma, dma, dma, dma, dma, dma, dma,
            dma, dma, dma,
        ],
        compiler_params=pltpu.CompilerParams(
            collective_id=0, has_side_effects=True, vmem_limit_bytes=48 * 1024 * 1024
        ),
    )(*[
        pltpu.with_memory_space_constraint(x, pltpu.HBM)
        for x in (thickness, u_layer, v_layer, tracers, sea_level, u_column, v_column, wet_cells, levels)
    ])
    return pl.pallas_call(
        store,
        out_shape=tuple(jax.ShapeDtypeStruct(shape, F32) for shape in shapes),
        in_specs=[near_spec] * 8,
        out_specs=(any_spec,) * 4,
        scratch_shapes=[vmem(NTR, 2, CY, CX), dma((NTR + 3,))],
    )(*[pltpu.with_memory_space_constraint(x, pltpu.VMEM) for x in results])


def solution(mesh):
    return jax.shard_map(
        body,
        mesh=mesh,
        in_specs=(
            P("depth", "tiles", None, None),
            P("depth", "tiles", None, None),
            P("depth", "tiles", None, None),
            P(None, "depth", "tiles", None, None),
            P("tiles", None, None),
            P("tiles", None, None),
            P("tiles", None, None),
            P("tiles", None, None),
            P("tiles", None, None),
        ),
        out_specs=(
            P(None, "depth", "tiles", None, None),
            P("tiles", None, None),
            P("tiles", None, None),
            P("tiles", None, None),
        ),
        check_vma=False,
    )
```

time: 512 us -> 33.4 us (0.07)
  starting transfers between devices: 272 us -> 0 us
  waiting for transfers between devices: 170 us -> 0 us
  Pallas kernels: 0 us -> 32.7 us
  other arithmetic: 26.6 us -> 0 us
  blocking collectives: 17.9 us -> 0 us
  between operations: 15.5 us -> 0.64 us
  local copies, waits for them, and re-layouts: 6.29 us -> 0 us
    ppermute x65 -> x0, starting transfers between devices: 272 us -> none  [the longest x36 190 us: shifted(): return lax.ppermute(value, axis, pairs)]
    ppermute x65 -> x0, waiting for transfers between devices: 96.1 us -> none  [the longest x36 67 us: shifted(): return lax.ppermute(value, axis, pairs)]
    psum x1 -> x0, waiting for transfers between devices: 73.9 us -> none  [body(): lax.psum((jnp.sum(flux_east, axis=0), jnp.sum(flux_north, axis=0), jnp.su...]
    pallas_call x0 -> x2, Pallas kernels: none -> 32.7 us  [the longest x1 31.6 us: body(): pl.pallas_call(kernel, out_shape=(vmem(NTR, 2, CY, CX), *(pltpu.VMEM(shap...]
    all_gather x1 -> x0, blocking collectives: 17.9 us -> none  [prefix(): everything = lax.all_gather(value, axis)]
  transfers between devices with their start and end apart: 66 -> 0, of which waited for: 39 -> 0; matrix products, arithmetic and copies ran while one was open for 4% -> 0% of each run, Pallas kernels for 0% -> 0%
where the time goes in v2:
time: 33.4 us; the launch traced here: 33.3 us
  Pallas kernels  32.7 us (98%)
  between operations  0.64 us (2%)
    pallas_call x1, Pallas kernels, body(): pl.pallas_call(kernel, out_shape=(vmem(NTR, 2, CY, CX), *(pltpu.VMEM(shap...  31.6 us
    pallas_call x1, Pallas kernels, body(): pl.pallas_call(store, out_shape=tuple((jax.ShapeDtypeStruct(shape, F32) f...  1.02 us

profile of v2, /device:TPU:1, one launch (start us, length us, event | category | flops | bytes accessed | tf_op | source)
XLA Modules:
  0.0 33.3 jit_solution(1351937325615628291)
XLA Ops:
  0.6 31.6 %shard_map.120 = (f32[6,2,128,128]{3,2,1,0:T(8,128)S(1)}, f32[1,128,128]{2,1,0:T(8,128)S(1)}, f32[1,128,128]{2,1,0:T(8,128)S(1)}, f32[1,128,128]{2,1,0:T(8,128)S...) custom-call(f32[2,1,128,128]{3,2,1,0:T(8,128)} %h_in.1, ...), custom_call_target="tpu_custom_call" | custom-call | tf_op jit(solution)/shard_map/pallas_call | solution.py:684
  32.3 1.0 %shard_map.121 = (f32[6,2,1,128,128]{4,3,2,1,0:T(8,128)}, f32[1,128,128]{2,1,0:T(8,128)}, f32[1,128,128]{2,1,0:T(8,128)}, f32[1,128,128]{2,1,0:T(8,128)}) custom-call(f32[6,2,128,128]{3,2,1,0:T(8,128)S(1)} %get-tuple-element.12.part, f32[1,128,128]{2,1,0:T(8,128)S(1)} %get-tuple-element.13.s_ref, f32[1,128,128]{2,1,0:T(8,128)S(1)} %get-tuple-element.14.e_ref, ...), custom_call_target="tpu_custom_call" | custom-call | tf_op jit(solution)/shard_map/pallas_call | solution.py:714

commit v3 on v2

--- a/solution.py
+++ b/solution.py
@@ -98,17 +98,20 @@
     def left(sem, rows):
         remote(sizes.at[0:rows], sizes.at[0:rows], sem, sem, member(partner)).wait_send()
 
-    for source, target in [
-        (h_in.at[:, 0], x.at[0:2, 0, rows_own]), (wet_in.at[0], wet), (lev_in.at[0], lev),
-        (u_in.at[:, 0], x.at[2:4, 0, rows_own]), (v_in.at[:, 0], x.at[4:6, 0, rows_own]),
-        (sea_in.at[0], state.at[0, 0, rows_own]), (uc_in.at[0], state.at[1, 0, rows_own]),
-        (vc_in.at[0], state.at[2, 0, rows_own]),
-    ]:
+    def fetch(source, target):
         pltpu.make_async_copy(source, target, loc_sem.at[0]).start()
 
+    fetch(h_in.at[:, 0], x.at[0:2, 0, rows_own])
+    fetch(wet_in.at[0], wet)
+    fetch(lev_in.at[0], lev)
+    fetch(u_in.at[:, 0], x.at[2:4, 0, rows_own])
+    fetch(v_in.at[:, 0], x.at[4:6, 0, rows_own])
     barrier = pltpu.get_barrier_semaphore()
     for dx, dy in around:
         pl.semaphore_signal(barrier, inc=1, device_id=beside(dx, dy), device_id_type=MESH)
+    fetch(sea_in.at[0], state.at[0, 0, rows_own])
+    fetch(uc_in.at[0], state.at[1, 0, rows_own])
+    fetch(vc_in.at[0], state.at[2, 0, rows_own])
     peers = [(me + k) % ND for k in range(1, ND)]
     for peer in peers:
         pl.semaphore_signal(barrier, inc=1, device_id=member(peer), device_id_type=MESH)
@@ -195,7 +198,7 @@
     rows_c = slice(8, CY + 8)
 
     def send_tracers(i):
-        part = slice(2 * i, 2 * i + 2)
+        part = slice(0, 2) if i == 0 else slice(2, NTR)
 
         @pl.when(me > 0)
         def _():
@@ -210,6 +213,13 @@
             ).start()
 
     send_tracers(0)
+
+    got(pair_got, 256)
+    chips = [(chip + k) % 4 for k in range(1, 4)]
+    for q in range(4):
+        chip_sum[q] = main_send[q, core] + pair_in[q]
+    for q in chips:
+        remote(chip_sum.at[q], main_in.at[chip], sent, rs_got, member(2 * q + core)).start()
 
     def pack_more(low, shift, east, west):
         old = state[1, 0, OWN + low : OWN + low + 8]
@@ -222,13 +232,6 @@
 
     pack_sides(1, late, pack_more)
 
-    got(pair_got, 256)
-    chips = [(chip + k) % 4 for k in range(1, 4)]
-    for q in range(4):
-        chip_sum[q] = main_send[q, core] + pair_in[q]
-    for q in chips:
-        remote(chip_sum.at[q], main_in.at[chip], sent, rs_got, member(2 * q + core)).start()
-    send_tracers(1)
     halo(1, side_pack.at[1, 0], side_in.at[1, 0], 1, 0)
     halo(1, side_pack.at[1, 1], side_in.at[1, 1], -1, 0)
     halo(1, state.at[:, 0, END - 16 : END], state.at[:, 0, 0:OWN], 0, 1)
@@ -398,7 +401,7 @@
         middle_chip = jnp.where(upper, 2, ND - 4)
         remote(outer_sum, outer_in, outer_sent, outer_got, member(middle_chip + core)).start()
 
-    send_tracers(2)
+    send_tracers(1)
 
     got(halo_got.at[1], 392)
 

time: 33.4 us -> 33.4 us (level)
  no operation moved by 1% of the time
where the time goes in v3:
time: 33.4 us; the launch traced here: 33.3 us
  Pallas kernels  32.7 us (98%)
  between operations  0.64 us (2%)
    pallas_call x1, Pallas kernels, body(): pl.pallas_call(kernel, out_shape=(vmem(NTR, 2, CY, CX), *(pltpu.VMEM(shap...  31.6 us
    pallas_call x1, Pallas kernels, body(): pl.pallas_call(store, out_shape=tuple((jax.ShapeDtypeStruct(shape, F32) f...  1.02 us

profile of v3, /device:TPU:1, one launch (start us, length us, event | category | flops | bytes accessed | tf_op | source)
XLA Modules:
  0.0 33.3 jit_solution(7358209300513390442)
XLA Ops:
  0.6 31.6 %shard_map.120 = (f32[6,2,128,128]{3,2,1,0:T(8,128)S(1)}, f32[1,128,128]{2,1,0:T(8,128)S(1)}, f32[1,128,128]{2,1,0:T(8,128)S(1)}, f32[1,128,128]{2,1,0:T(8,128)S...) custom-call(f32[2,1,128,128]{3,2,1,0:T(8,128)} %h_in.1, ...), custom_call_target="tpu_custom_call" | custom-call | tf_op jit(solution)/shard_map/pallas_call | solution.py:687
  32.3 1.0 %shard_map.121 = (f32[6,2,1,128,128]{4,3,2,1,0:T(8,128)}, f32[1,128,128]{2,1,0:T(8,128)}, f32[1,128,128]{2,1,0:T(8,128)}, f32[1,128,128]{2,1,0:T(8,128)}) custom-call(f32[6,2,128,128]{3,2,1,0:T(8,128)S(1)} %get-tuple-element.12.part, f32[1,128,128]{2,1,0:T(8,128)S(1)} %get-tuple-element.13.s_ref, f32[1,128,128]{2,1,0:T(8,128)S(1)} %get-tuple-element.14.e_ref, ...), custom_call_target="tpu_custom_call" | custom-call | tf_op jit(solution)/shard_map/pallas_call | solution.py:717

commit v4 on v3

--- a/solution.py
+++ b/solution.py
@@ -55,9 +55,9 @@
     main_send, pair_in, chip_sum, main_in, main_all,
     edge_send, edge_in, edge_all,
     face_e, face_n, local, total,
-    tw, ae, an, be, bn, ce, cn,
+    tw, ae, an, be, bn, ce, cn, wet_e_all, wet_n_all, state_b,
     outer_send, outer_pair, outer_sum, outer_in, outer_div,
-    flow_n, flow_t, prod_n, coef, div_1, whole_div, pair_send, pair_div,
+    flow_n, flow_t, flow_w, flow_e, prod_n, coef, div_1, whole_div, pair_send, pair_div,
     loc_sem, sent, sent_late, edge_sent, outer_sent, up_sent, down_sent,
     halo_got, pair_got, rs_got, ag_got, forward_got, edge_got, edge_all_got, half_got, outer_got,
     up_got, down_got, div_got,
@@ -101,14 +101,14 @@
     def fetch(source, target):
         pltpu.make_async_copy(source, target, loc_sem.at[0]).start()
 
+    barrier = pltpu.get_barrier_semaphore()
+    for dx, dy in around:
+        pl.semaphore_signal(barrier, inc=1, device_id=beside(dx, dy), device_id_type=MESH)
     fetch(h_in.at[:, 0], x.at[0:2, 0, rows_own])
     fetch(wet_in.at[0], wet)
     fetch(lev_in.at[0], lev)
     fetch(u_in.at[:, 0], x.at[2:4, 0, rows_own])
     fetch(v_in.at[:, 0], x.at[4:6, 0, rows_own])
-    barrier = pltpu.get_barrier_semaphore()
-    for dx, dy in around:
-        pl.semaphore_signal(barrier, inc=1, device_id=beside(dx, dy), device_id_type=MESH)
     fetch(sea_in.at[0], state.at[0, 0, rows_own])
     fetch(uc_in.at[0], state.at[1, 0, rows_own])
     fetch(vc_in.at[0], state.at[2, 0, rows_own])
@@ -251,6 +251,7 @@
         for k in range(2):
             ref[:, k, HIGH:RX] = jnp.zeros((ref.shape[0], RX - HIGH, CX), F32)
     state[2, 1, 0:LOW] = jnp.zeros((LOW, CX), F32)
+    state_b[2, :, 0:LOW] = jnp.zeros((2, LOW, CX), F32)
 
     has_n = ty < TROWS - 1
     has_s = ty > 0
@@ -356,6 +357,15 @@
         for q in chips + [chip]:
             remote(edge_send.at[q], edge_in.at[me], edge_sent, edge_got, member(2 * q)).start()
 
+    got(rs_got, 192)
+    mine = chip_sum[chip]
+    for q in chips:
+        mine = mine + main_in[q]
+    main_all[chip, core] = mine
+    piece = main_all.at[chip, core]
+    for q in chips:
+        remote(piece, piece, sent, ag_got, member(2 * q + core)).start()
+
     @pl.when(outer)
     def _():
         for i in range(4):
@@ -375,15 +385,6 @@
             outer_send[j, 200:208] = block
         remote(outer_send.at[other], outer_pair, outer_sent, half_got, member(partner)).start()
 
-    got(rs_got, 192)
-    mine = chip_sum[chip]
-    for q in chips:
-        mine = mine + main_in[q]
-    main_all[chip, core] = mine
-    piece = main_all.at[chip, core]
-    for q in chips:
-        remote(piece, piece, sent, ag_got, member(2 * q + core)).start()
-
     @pl.when(owner)
     def _():
         got(edge_got, 7 * 8 * EB)
@@ -430,8 +431,8 @@
             tw[k, here] = tau * is_wet[k]
             ae[k, here] = (1.0 - tau) * (is_wet[k] * wet_e[k])
             an[k, here] = (1.0 - tau) * (is_wet[k] * wet_n[k])
-            be[k, here] = (tau * coupling) * (is_wet[k] * wet_e[k])
-            bn[k, here] = (tau * coupling) * (is_wet[k] * wet_n[k])
+            wet_e_all[k, here] = (tau * coupling) * (is_wet[k] * wet_e[k])
+            wet_n_all[k, here] = (tau * coupling) * (is_wet[k] * wet_n[k])
 
     got(ag_got, 192)
     half = main_all.at[:, core]
@@ -450,62 +451,76 @@
     def block_of(i):
         return edge_all[i // EB, 8 * (i % EB) : 8 * (i % EB) + 8]
 
-    for f in range(4):
-        for p in range(ND):
-            low = OWN + 16 * p
-            total[f, 0, low : low + 16] = main_all[p // 2, p % 2, 16 * f : 16 * f + 16]
-        total[f, 0, END - 1 : END + 7] = block_of(9 + f)
-        total[f, 0, HIGH - 1 : HIGH] = jnp.zeros((1, CX), F32)
-        total[f, 0, LOW:OWN] = block_of(13 + f)
     rim = (lane8 < 7) | (lane8 >= CX - 8)
+    last_lane = lane8 == CX - 1
+    row8 = rows_of(8)
     for i in range(18):
         block = block_of(i % 9)
         shift = 64 * (i // 9)
         here = slice(LOW + 8 * i, LOW + 8 * i + 8)
+        sums = []
         for f in range(4):
-            edge = jnp.where(lane8 == CX - 1, roll(block, CX - 1 - 16 * f - shift, 1), total[f, 0, here])
+            if i == 0:
+                main = block_of(13 + f)
+            elif i == 17:
+                main = jnp.where(row8 == 7, 0.0, roll(block_of(9 + f), -1, 0))
+            else:
+                p, part_low = (i - 1) // 2, 16 * f + 8 * ((i - 1) % 2)
+                main = main_all[p // 2, p % 2, part_low : part_low + 8]
+                if i == 16:
+                    main = jnp.where(row8 == 7, jnp.broadcast_to(block_of(9 + f)[0:1], (8, CX)), main)
+            main = jnp.where(last_lane, roll(block, CX - 1 - 16 * f - shift, 1), main)
             side = jnp.where(rim, roll(block, -(9 + 16 * f + shift), 1), 0.0)
-            total[f, 0, here] = edge
+            total[f, 0, here] = main
             total[f, 1, here] = side
-            for k, value in enumerate((edge, side)):
-                if f == 2:
-                    ce[k, here] = be[k, here] * value
-                if f == 3:
-                    cn[k, here] = bn[k, here] * value
+            sums.append((main, side))
         for k in range(2):
-            be[k, here] = be[k, here] * total[0, k, here]
-            bn[k, here] = bn[k, here] * total[1, k, here]
-
-    def substep(i, carry):
+            east, north = wet_e_all[k, here], wet_n_all[k, here]
+            be[k, here] = east * sums[0][k]
+            bn[k, here] = north * sums[1][k]
+            ce[k, here] = east * sums[2][k]
+            cn[k, here] = north * sums[3][k]
+
+    def substep(old, new):
+        bottom_row = rows_of(step) == step - 1
+
         def rise(low):
             here = slice(low, low + step)
-            east = both(state.at[1], low, step)
+            east = both(old.at[1], low, step)
             west = shifted(east, 1)
-            north = both(state.at[2], low, step)
-            south = both(state.at[2], low - 1, step)
+            north = both(old.at[2], low, step)
+            south = both(old.at[2], low - 1, step)
             level = []
             for k in range(2):
-                value = state[0, k, here] - tw[k, here] * (east[k] - west[k] + north[k] - south[k])
-                state[0, k, here] = value
+                value = old[0, k, here] - tw[k, here] * (east[k] - west[k] + north[k] - south[k])
+                new[0, k, here] = value
                 level.append(value)
             return level, east, north
 
-        def move(low, level, east, north):
+        def move(low, held, beyond):
             here = slice(low, low + step)
+            level, east, north = held
             level_e = shifted(level, -1)
-            level_n = both(state.at[0], low + 1, step)
             for k in range(2):
-                state[1, k, here] = ae[k, here] * east[k] - be[k, here] * (level_e[k] - level[k]) + ce[k, here]
-                state[2, k, here] = an[k, here] * north[k] - bn[k, here] * (level_n[k] - level[k]) + cn[k, here]
+                level_n = roll(level[k], -1, 0)
+                if beyond is not None:
+                    first_row = jnp.broadcast_to(beyond[0][k][0:1], (step, CX))
+                    level_n = jnp.where(bottom_row, first_row, level_n)
+                new[1, k, here] = ae[k, here] * east[k] - be[k, here] * (level_e[k] - level[k]) + ce[k, here]
+                new[2, k, here] = an[k, here] * north[k] - bn[k, here] * (level_n - level[k]) + cn[k, here]
 
         held = rise(LOW)
         for low in range(LOW, HIGH, step):
             coming = rise(low + step) if low + step < HIGH else None
-            move(low, *held)
+            move(low, held, coming)
             held = coming
+
+    def two(i, carry):
+        substep(state, state_b)
+        substep(state_b, state)
         return carry
 
-    lax.fori_loop(0, NSUB, substep, 0)
+    lax.fori_loop(0, NSUB // 2, two, 0)
 
     flow_rows = [(OWN - 8, 8)] + [(OWN + 32 * i, 32) for i in range(4)]
     for low, size in flow_rows:
@@ -513,7 +528,6 @@
         shift_n = state[2, 0, here] - coupling * total[3, 0, here]
         for l in range(2):
             flow_n[l, here] = face_n[l, 0, here] * (x[4 + l, 0, here] + shift_n)
-        flow_t[here] = total[3, 0, here] + total[1, 0, here] * shift_n
         prod_n[here] = shift_n
 
     for i in range(4):
@@ -521,26 +535,13 @@
         here = slice(low, low + 32)
         mine = slice(32 * i, 32 * i + 32)
         shift_e = [state[1, k, here] - coupling * total[2, k, here] for k in range(2)]
-        flow = [total[2, k, here] + total[0, k, here] * shift_e[k] for k in range(2)]
-        whole_div[mine] = flow[0] - shifted(flow, 1)[0] + flow_t[here] - flow_t[low - 1 : low + 31]
-        count = x[6, 0, here]
         divs = []
         for l in range(2):
             flow = [face_e[l, k, here] * (x[2 + l, k, here] + shift_e[k]) for k in range(2)]
-            fe = flow[0]
-            fw = shifted(flow, 1)[0]
-            fn = flow_n[l, here]
-            fs = flow_n[l, low - 1 : low + 31]
-            divs.append(fe - fw + fn - fs)
-            gain = jnp.where(first + l < count, tracer_time / x[l, 0, here], 0.0)
-            plus_e, minus_w = jnp.maximum(fe, 0.0), jnp.minimum(fw, 0.0)
-            plus_n, minus_s = jnp.maximum(fn, 0.0), jnp.minimum(fs, 0.0)
-            coef[l, 0, mine] = gain * (plus_e - fe)
-            coef[l, 1, mine] = gain * (fw - minus_w)
-            coef[l, 2, mine] = gain * (plus_n - fn)
-            coef[l, 3, mine] = gain * (fs - minus_s)
-            coef[l, 4, mine] = 1.0 - gain * (plus_e - minus_w + plus_n - minus_s)
-            coef[l, 5, mine] = gain
+            west = shifted(flow, 1)[0]
+            flow_e[l, 0, mine] = flow[0]
+            flow_e[l, 1, mine] = west
+            divs.append(flow[0] - west + flow_n[l, here] - flow_n[l, low - 1 : low + 31])
         div_1[mine] = divs[1]
         pair_send[mine] = divs[0] + divs[1]
 
@@ -560,6 +561,31 @@
         pair_send[CY : CY + 64] = value
 
     remote(pair_send, pair_div, sent, div_got, member(partner)).start()
+
+    for low, size in flow_rows:
+        here = slice(low, low + size)
+        flow_w[here] = total[3, 0, here] + total[1, 0, here] * prod_n[here]
+
+    for i in range(4):
+        low = OWN + 32 * i
+        here = slice(low, low + 32)
+        mine = slice(32 * i, 32 * i + 32)
+        shift_e = [state[1, k, here] - coupling * total[2, k, here] for k in range(2)]
+        flow = [total[2, k, here] + total[0, k, here] * shift_e[k] for k in range(2)]
+        whole_div[mine] = flow[0] - shifted(flow, 1)[0] + flow_w[here] - flow_w[low - 1 : low + 31]
+        count = x[6, 0, here]
+        for l in range(2):
+            fe, fw = flow_e[l, 0, mine], flow_e[l, 1, mine]
+            fn, fs = flow_n[l, here], flow_n[l, low - 1 : low + 31]
+            gain = jnp.where(first + l < count, tracer_time / x[l, 0, here], 0.0)
+            plus_e, minus_w = jnp.maximum(fe, 0.0), jnp.minimum(fw, 0.0)
+            plus_n, minus_s = jnp.maximum(fn, 0.0), jnp.minimum(fs, 0.0)
+            coef[l, 0, mine] = gain * (plus_e - fe)
+            coef[l, 1, mine] = gain * (fw - minus_w)
+            coef[l, 2, mine] = gain * (plus_n - fn)
+            coef[l, 3, mine] = gain * (fs - minus_s)
+            coef[l, 4, mine] = 1.0 - gain * (plus_e - minus_w + plus_n - minus_s)
+            coef[l, 5, mine] = gain
 
     s_out[0] = state[0, 0, rows_own]
     e_out[0] = state[1, 0, rows_own]
@@ -699,9 +725,9 @@
             halves, quarter, quarter, quarter, halves,
             edges, vmem(ND, 8 * EB, CX), edges,
             wide2, wide2, vmem(4, 2, RX, CX), vmem(4, 2, RX, CX),
-            wide, wide, wide, wide, wide, wide, wide,
+            wide, wide, wide, wide, wide, wide, wide, wide, wide, vmem(3, 2, RX, CX),
             vmem(2, 208, CX), vmem(208, CX), vmem(208, CX), vmem(208, CX), vmem(2, 64, CX),
-            vmem(2, RX, CX), vmem(RX, CX), vmem(RX, CX), vmem(2, 6, CY, CX),
+            vmem(2, RX, CX), vmem(RX, CX), vmem(RX, CX), vmem(2, 2, CY, CX), vmem(RX, CX), vmem(2, 6, CY, CX),
             plane, plane, vmem(CY + 64, CX), vmem(CY + 64, CX),
             dma((2,)), dma, dma, dma, dma, dma, dma,
             dma((2,)), dma, dma, dma, dma, dma, dma, dma, dma,

time: 33.4 us -> 33.1 us (level)
  Pallas kernels: 32.7 us -> 32.3 us
where the time goes in v4:
time: 33.1 us; the launch traced here: 33 us
  Pallas kernels  32.3 us (98%)
  between operations  0.64 us (2%)
    pallas_call x1, Pallas kernels, body(): pl.pallas_call(kernel, out_shape=(vmem(NTR, 2, CY, CX), *(pltpu.VMEM(shap...  31.3 us
    pallas_call x1, Pallas kernels, body(): pl.pallas_call(store, out_shape=tuple((jax.ShapeDtypeStruct(shape, F32) f...  1.02 us

profile of v4, /device:TPU:1, one launch (start us, length us, event | category | flops | bytes accessed | tf_op | source)
XLA Modules:
  0.0 33.0 jit_solution(11193066058785290523)
XLA Ops:
  0.6 31.3 %shard_map.120 = (f32[6,2,128,128]{3,2,1,0:T(8,128)S(1)}, f32[1,128,128]{2,1,0:T(8,128)S(1)}, f32[1,128,128]{2,1,0:T(8,128)S(1)}, f32[1,128,128]{2,1,0:T(8,128)S...) custom-call(f32[2,1,128,128]{3,2,1,0:T(8,128)} %h_in.1, ...), custom_call_target="tpu_custom_call" | custom-call | tf_op jit(solution)/shard_map/pallas_call | solution.py:713
  32.0 1.0 %shard_map.121 = (f32[6,2,1,128,128]{4,3,2,1,0:T(8,128)}, f32[1,128,128]{2,1,0:T(8,128)}, f32[1,128,128]{2,1,0:T(8,128)}, f32[1,128,128]{2,1,0:T(8,128)}) custom-call(f32[6,2,128,128]{3,2,1,0:T(8,128)S(1)} %get-tuple-element.12.part, f32[1,128,128]{2,1,0:T(8,128)S(1)} %get-tuple-element.13.s_ref, f32[1,128,128]{2,1,0:T(8,128)S(1)} %get-tuple-element.14.e_ref, ...), custom_call_target="tpu_custom_call" | custom-call | tf_op jit(solution)/shard_map/pallas_call | solution.py:743

commit v5 on v4

--- a/solution.py
+++ b/solution.py
@@ -89,7 +89,10 @@
             device_id=where, device_id_type=MESH,
         )
 
-    around = [(1, 0), (-1, 0), (0, 1), (0, -1), (1, 1), (-1, 1), (1, -1), (-1, -1)]
+    has_n = ty < TROWS - 1
+    has_s = ty > 0
+    inner = has_n & has_s
+
     rows_own = slice(OWN, END)
 
     def got(sem, rows):
@@ -102,8 +105,21 @@
         pltpu.make_async_copy(source, target, loc_sem.at[0]).start()
 
     barrier = pltpu.get_barrier_semaphore()
-    for dx, dy in around:
-        pl.semaphore_signal(barrier, inc=1, device_id=beside(dx, dy), device_id_type=MESH)
+
+    def greet(dy):
+        for dx in (1, -1) if dy == 0 else (0, 1, -1):
+            pl.semaphore_signal(barrier, inc=1, device_id=beside(dx, dy), device_id_type=MESH)
+
+    greet(0)
+
+    @pl.when(has_n)
+    def _():
+        greet(1)
+
+    @pl.when(has_s)
+    def _():
+        greet(-1)
+
     fetch(h_in.at[:, 0], x.at[0:2, 0, rows_own])
     fetch(wet_in.at[0], wet)
     fetch(lev_in.at[0], lev)
@@ -152,7 +168,13 @@
         corner_pack[0, j] = east
         corner_pack[1, j] = west
 
-    pl.semaphore_wait(barrier, len(around) + ND - 1)
+    @pl.when(inner)
+    def _():
+        pl.semaphore_wait(barrier, 8 + ND - 1)
+
+    @pl.when(jnp.logical_not(inner))
+    def _():
+        pl.semaphore_wait(barrier, 5 + ND - 1)
 
     def halo(phase, source, target, dx, dy):
         sem = sent if phase == 0 else sent_late
@@ -160,12 +182,18 @@
 
     halo(0, side_pack.at[0, 0], side_in.at[0, 0], 1, 0)
     halo(0, side_pack.at[0, 1], side_in.at[0, 1], -1, 0)
-    halo(0, corner_pack.at[0, 1], corner_in.at[0], 1, 1)
-    halo(0, corner_pack.at[1, 1], corner_in.at[1], -1, 1)
-    halo(0, corner_pack.at[0, 0], corner_in.at[2], 1, -1)
-    halo(0, corner_pack.at[1, 0], corner_in.at[3], -1, -1)
-    halo(0, x.at[:, 0, END - 8 : END], x.at[:, 0, LOW:OWN], 0, 1)
-    halo(0, x.at[:, 0, OWN : OWN + 8], x.at[:, 0, END:HIGH], 0, -1)
+
+    @pl.when(has_n)
+    def _():
+        halo(0, corner_pack.at[0, 1], corner_in.at[0], 1, 1)
+        halo(0, corner_pack.at[1, 1], corner_in.at[1], -1, 1)
+        halo(0, x.at[:, 0, END - 8 : END], x.at[:, 0, LOW:OWN], 0, 1)
+
+    @pl.when(has_s)
+    def _():
+        halo(0, corner_pack.at[0, 0], corner_in.at[2], 1, -1)
+        halo(0, corner_pack.at[1, 0], corner_in.at[3], -1, -1)
+        halo(0, x.at[:, 0, OWN : OWN + 8], x.at[:, 0, END:HIGH], 0, -1)
 
     first = (2 * me).astype(F32)
     lane16 = lanes(16)
@@ -234,10 +262,16 @@
 
     halo(1, side_pack.at[1, 0], side_in.at[1, 0], 1, 0)
     halo(1, side_pack.at[1, 1], side_in.at[1, 1], -1, 0)
-    halo(1, state.at[:, 0, END - 16 : END], state.at[:, 0, 0:OWN], 0, 1)
-    halo(1, state.at[:, 0, OWN : OWN + 8], state.at[:, 0, END:HIGH], 0, -1)
-    halo(1, c.at[:, :, CY : CY + 8], c.at[:, :, 0:8], 0, 1)
-    halo(1, c.at[:, :, 8:16], c.at[:, :, CY + 8 : CY + 16], 0, -1)
+
+    @pl.when(has_n)
+    def _():
+        halo(1, state.at[:, 0, END - 16 : END], state.at[:, 0, 0:OWN], 0, 1)
+        halo(1, c.at[:, :, CY : CY + 8], c.at[:, :, 0:8], 0, 1)
+
+    @pl.when(has_s)
+    def _():
+        halo(1, state.at[:, 0, OWN : OWN + 8], state.at[:, 0, END:HIGH], 0, -1)
+        halo(1, c.at[:, :, 8:16], c.at[:, :, CY + 8 : CY + 16], 0, -1)
 
     @pl.when(me == 0)
     def _():
@@ -252,9 +286,6 @@
             ref[:, k, HIGH:RX] = jnp.zeros((ref.shape[0], RX - HIGH, CX), F32)
     state[2, 1, 0:LOW] = jnp.zeros((LOW, CX), F32)
     state_b[2, :, 0:LOW] = jnp.zeros((2, LOW, CX), F32)
-
-    has_n = ty < TROWS - 1
-    has_s = ty > 0
 
     def unpack_sides(phase, fields, extra=None):
         side = (lane8 < 8) | (lane8 >= CX - 8)
@@ -278,7 +309,14 @@
             if extra is not None and 0 <= i < 16:
                 extra(8 * i, shift, west, east)
 
-    got(halo_got.at[0], 272)
+    @pl.when(inner)
+    def _():
+        got(halo_got.at[0], 272)
+
+    @pl.when(jnp.logical_not(inner))
+    def _():
+        got(halo_got.at[0], 200)
+
     unpack_sides(0, [x.at[f, 1] for f in range(7)])
 
     @pl.when(jnp.logical_not(has_s))
@@ -383,7 +421,7 @@
                 turned = roll(local[0, 1, low + 8 * r : low + 8 * r + 8], r + 1, 1)
                 block = jnp.where(lane8 == r, turned, block)
             outer_send[j, 200:208] = block
-        remote(outer_send.at[other], outer_pair, outer_sent, half_got, member(partner)).start()
+        remote(outer_send, outer_pair, outer_sent, half_got, member(partner)).start()
 
     @pl.when(owner)
     def _():
@@ -397,14 +435,28 @@
 
     @pl.when(outer)
     def _():
-        got(half_got, 208)
-        outer_sum[...] = outer_send[core] + outer_pair[...]
+        got(half_got, 416)
+        outer_sum[...] = outer_send[core] + outer_pair[core]
         middle_chip = jnp.where(upper, 2, ND - 4)
         remote(outer_sum, outer_in, outer_sent, outer_got, member(middle_chip + core)).start()
 
     send_tracers(1)
 
-    got(halo_got.at[1], 392)
+    @pl.when(inner)
+    def _():
+        got(halo_got.at[1], 392)
+        left(sent_late, 392)
+
+    @pl.when(jnp.logical_not(has_s))
+    def _():
+        got(halo_got.at[1], 248)
+        left(sent_late, 272)
+
+    @pl.when(jnp.logical_not(has_n))
+    def _():
+        got(halo_got.at[1], 272)
+        left(sent_late, 248)
+
 
     def put_tracers(low, shift, west, east):
         for p in range(2 * NTR):
@@ -412,15 +464,16 @@
             edge_c[p // 2, p % 2, low : low + 8] = roll(value, 79 - shift - p, 1)
 
     unpack_sides(1, [state.at[f, 1] for f in range(3)], put_tracers)
-    left(sent_late, 392)
 
     @pl.when(jnp.logical_not(has_s))
     def _():
-        state[:, 0, LOW:OWN] = jnp.zeros((3, 8, CX), F32)
+        state[:, 0, 0:OWN] = jnp.zeros((3, OWN, CX), F32)
+        c[:, :, 0:8] = jnp.zeros((NTR, 2, 8, CX), F32)
 
     @pl.when(jnp.logical_not(has_n))
     def _():
         state[:, 0, END:HIGH] = jnp.zeros((3, 8, CX), F32)
+        c[:, :, CY + 8 : CY + 16] = jnp.zeros((NTR, 2, 8, CX), F32)
 
     for low in range(LOW, HIGH, step):
         here = slice(low, low + step)
@@ -545,22 +598,29 @@
         div_1[mine] = divs[1]
         pair_send[mine] = divs[0] + divs[1]
 
-    @pl.when(jnp.logical_not(outer))
-    def _():
-        got(outer_got, 208)
-        base = pl.multiple_of(OWN + 64 * core, 8)
+    def divergence_of(parts, base):
         here = pl.ds(base, 64)
         shift_e = [state[1, k, here] - coupling * total[2, k, here] for k in range(2)]
-        flow = outer_in[64:128] * shift_e[0]
-        block = outer_in[200:208]
+        flow = parts[64:128] * shift_e[0]
+        block = parts[200:208]
         column = jnp.concatenate([roll(block, -r, 1) for r in range(8)], axis=0)
         west = jnp.where(lanes(64) == 0, column * roll(shift_e[1], 1, 1), roll(flow, 1, 1))
-        flow_t[0:72] = outer_in[128:200] * prod_n[pl.ds(pl.multiple_of(base - 8, 8), 72)]
-        value = outer_in[0:64] + flow - west + flow_t[8:72] - flow_t[7:71]
+        flow_t[0:72] = parts[128:200] * prod_n[pl.ds(base - 8, 72)]
+        return parts[0:64] + flow - west + flow_t[8:72] - flow_t[7:71]
+
+    @pl.when(jnp.logical_not(outer))
+    def _():
+        got(outer_got, 208)
+        value = divergence_of(outer_in, pl.multiple_of(OWN + 64 * core, 8))
         outer_div[core] = value
         pair_send[CY : CY + 64] = value
-
-    remote(pair_send, pair_div, sent, div_got, member(partner)).start()
+        remote(pair_send, pair_div, sent, div_got, member(partner)).start()
+
+    @pl.when(outer)
+    def _():
+        for j in range(2):
+            pair_div[64 * j : 64 * j + 64] = divergence_of(outer_pair.at[j], OWN + 64 * j)
+        outer_div[...] = jnp.zeros_like(outer_div)
 
     for low, size in flow_rows:
         here = slice(low, low + size)
@@ -610,7 +670,15 @@
                     + a_s * c[m, l, low - 1 : low + 31]
                 )
 
-    left(sent, 1360)
+    halos_sent = [(inner, 272), (jnp.logical_not(inner), 200)]
+    for where, rows in halos_sent:
+        @pl.when(where & outer)
+        def _(rows=rows):
+            left(sent, rows + 896)
+
+        @pl.when(where & jnp.logical_not(outer))
+        def _(rows=rows):
+            left(sent, rows + 1088)
 
     @pl.when(owner)
     def _():
@@ -622,17 +690,12 @@
 
     @pl.when(outer)
     def _():
-        left(outer_sent, 416)
-
-    got(div_got, 192)
+        left(outer_sent, 624)
 
     @pl.when(jnp.logical_not(outer))
     def _():
+        got(div_got, 192)
         outer_div[other] = pair_div[CY : CY + 64]
-
-    @pl.when(outer)
-    def _():
-        outer_div[...] = jnp.zeros_like(outer_div)
 
     odd = core == 1
     for i in range(4):
@@ -726,7 +789,7 @@
             edges, vmem(ND, 8 * EB, CX), edges,
             wide2, wide2, vmem(4, 2, RX, CX), vmem(4, 2, RX, CX),
             wide, wide, wide, wide, wide, wide, wide, wide, wide, vmem(3, 2, RX, CX),
-            vmem(2, 208, CX), vmem(208, CX), vmem(208, CX), vmem(208, CX), vmem(2, 64, CX),
+            vmem(2, 208, CX), vmem(2, 208, CX), vmem(208, CX), vmem(208, CX), vmem(2, 64, CX),
             vmem(2, RX, CX), vmem(RX, CX), vmem(RX, CX), vmem(2, 2, CY, CX), vmem(RX, CX), vmem(2, 6, CY, CX),
             plane, plane, vmem(CY + 64, CX), vmem(CY + 64, CX),
             dma((2,)), dma, dma, dma, dma, dma, dma,

time: 33.1 us -> 32.1 us (0.970)
  the two profiles are of different devices: /device:TPU:1 before, /device:TPU:35 now
where the time goes in v5:
time: 32.1 us; the launch traced here: 32 us
  Pallas kernels  31.4 us (98%)
  between operations  0.64 us (2%)
    pallas_call x1, Pallas kernels, body(): pl.pallas_call(kernel, out_shape=(vmem(NTR, 2, CY, CX), *(pltpu.VMEM(shap...  30.3 us
    pallas_call x1, Pallas kernels, body(): pl.pallas_call(store, out_shape=tuple((jax.ShapeDtypeStruct(shape, F32) f...  1.02 us

profile of v5, /device:TPU:35, one launch (start us, length us, event | category | flops | bytes accessed | tf_op | source)
XLA Modules:
  0.0 32.0 jit_solution(15597546347013481047)
XLA Ops:
  0.6 30.3 %shard_map.120 = (f32[6,2,128,128]{3,2,1,0:T(8,128)S(1)}, f32[1,128,128]{2,1,0:T(8,128)S(1)}, f32[1,128,128]{2,1,0:T(8,128)S(1)}, f32[1,128,128]{2,1,0:T(8,128)S...) custom-call(f32[2,1,128,128]{3,2,1,0:T(8,128)} %h_in.1, ...), custom_call_target="tpu_custom_call" | custom-call | tf_op jit(solution)/shard_map/pallas_call | solution.py:776
  31.0 1.0 %shard_map.121 = (f32[6,2,1,128,128]{4,3,2,1,0:T(8,128)}, f32[1,128,128]{2,1,0:T(8,128)}, f32[1,128,128]{2,1,0:T(8,128)}, f32[1,128,128]{2,1,0:T(8,128)}) custom-call(f32[6,2,128,128]{3,2,1,0:T(8,128)S(1)} %get-tuple-element.12.part, f32[1,128,128]{2,1,0:T(8,128)S(1)} %get-tuple-element.13.s_ref, f32[1,128,128]{2,1,0:T(8,128)S(1)} %get-tuple-element.14.e_ref, ...), custom_call_target="tpu_custom_call" | custom-call | tf_op jit(solution)/shard_map/pallas_call | solution.py:806

commit v6 on v5

--- a/solution.py
+++ b/solution.py
@@ -52,14 +52,14 @@
     x, state, wet, lev,
     side_pack, side_in, corner_pack, corner_in, sizes,
     edge_c,
-    main_send, pair_in, chip_sum, main_in, main_all,
+    main_send, main_in, main_all,
     edge_send, edge_in, edge_all,
     face_e, face_n, local, total,
     tw, ae, an, be, bn, ce, cn, wet_e_all, wet_n_all, state_b,
     outer_send, outer_pair, outer_sum, outer_in, outer_div,
     flow_n, flow_t, flow_w, flow_e, prod_n, coef, div_1, whole_div, pair_send, pair_div,
     loc_sem, sent, sent_late, edge_sent, outer_sent, up_sent, down_sent,
-    halo_got, pair_got, rs_got, ag_got, forward_got, edge_got, edge_all_got, half_got, outer_got,
+    halo_got, rs_got, ag_got, forward_got, edge_got, edge_all_got, half_got, outer_got,
     up_got, down_got, div_got,
 ):
     me = lax.axis_index("depth")
@@ -168,33 +168,6 @@
         corner_pack[0, j] = east
         corner_pack[1, j] = west
 
-    @pl.when(inner)
-    def _():
-        pl.semaphore_wait(barrier, 8 + ND - 1)
-
-    @pl.when(jnp.logical_not(inner))
-    def _():
-        pl.semaphore_wait(barrier, 5 + ND - 1)
-
-    def halo(phase, source, target, dx, dy):
-        sem = sent if phase == 0 else sent_late
-        remote(source, target, sem, halo_got.at[phase], beside(dx, dy)).start()
-
-    halo(0, side_pack.at[0, 0], side_in.at[0, 0], 1, 0)
-    halo(0, side_pack.at[0, 1], side_in.at[0, 1], -1, 0)
-
-    @pl.when(has_n)
-    def _():
-        halo(0, corner_pack.at[0, 1], corner_in.at[0], 1, 1)
-        halo(0, corner_pack.at[1, 1], corner_in.at[1], -1, 1)
-        halo(0, x.at[:, 0, END - 8 : END], x.at[:, 0, LOW:OWN], 0, 1)
-
-    @pl.when(has_s)
-    def _():
-        halo(0, corner_pack.at[0, 0], corner_in.at[2], 1, -1)
-        halo(0, corner_pack.at[1, 0], corner_in.at[3], -1, -1)
-        halo(0, x.at[:, 0, OWN : OWN + 8], x.at[:, 0, END:HIGH], 0, -1)
-
     first = (2 * me).astype(F32)
     lane16 = lanes(16)
     row16 = rows_of(16)
@@ -219,8 +192,37 @@
             new = [de, dn, x[2 + l, 0, here] * de, x[4 + l, 0, here] * dn]
             sums = [a + b for a, b in zip(sums, new)]
         for f in range(4):
-            main_send[p // 2, p % 2, 16 * f : 16 * f + 16] = sums[f]
-    remote(main_send.at[:, other], pair_in, sent, pair_got, member(partner)).start()
+            main_send[p, 16 * f : 16 * f + 16] = sums[f]
+    @pl.when(inner)
+    def _():
+        pl.semaphore_wait(barrier, 8 + ND - 1)
+
+    @pl.when(jnp.logical_not(inner))
+    def _():
+        pl.semaphore_wait(barrier, 5 + ND - 1)
+
+    def halo(phase, source, target, dx, dy):
+        sem = sent if phase == 0 else sent_late
+        remote(source, target, sem, halo_got.at[phase], beside(dx, dy)).start()
+
+    halo(0, side_pack.at[0, 0], side_in.at[0, 0], 1, 0)
+    halo(0, side_pack.at[0, 1], side_in.at[0, 1], -1, 0)
+
+    @pl.when(has_n)
+    def _():
+        halo(0, corner_pack.at[0, 1], corner_in.at[0], 1, 1)
+        halo(0, corner_pack.at[1, 1], corner_in.at[1], -1, 1)
+        halo(0, x.at[:, 0, END - 8 : END], x.at[:, 0, LOW:OWN], 0, 1)
+
+    @pl.when(has_s)
+    def _():
+        halo(0, corner_pack.at[0, 0], corner_in.at[2], 1, -1)
+        halo(0, corner_pack.at[1, 0], corner_in.at[3], -1, -1)
+        halo(0, x.at[:, 0, OWN : OWN + 8], x.at[:, 0, END:HIGH], 0, -1)
+
+    far_first = [(me + k) % ND for k in (4, 5, 3, 2, 6, 7, 1)]
+    for peer in far_first:
+        remote(main_send.at[peer], main_in.at[me], sent, rs_got, member(peer)).start()
 
     fetch_c.wait()
     rows_c = slice(8, CY + 8)
@@ -242,13 +244,7 @@
 
     send_tracers(0)
 
-    got(pair_got, 256)
-    chips = [(chip + k) % 4 for k in range(1, 4)]
-    for q in range(4):
-        chip_sum[q] = main_send[q, core] + pair_in[q]
-    for q in chips:
-        remote(chip_sum.at[q], main_in.at[chip], sent, rs_got, member(2 * q + core)).start()
-
+    chips = [(chip + k) % 4 for k in (2, 1, 3)]
     def pack_more(low, shift, east, west):
         old = state[1, 0, OWN + low : OWN + low + 8]
         east = jnp.where(between(lane8, shift + 24, shift + 32), roll(old, 40 + shift, 1), east)
@@ -395,10 +391,10 @@
         for q in chips + [chip]:
             remote(edge_send.at[q], edge_in.at[me], edge_sent, edge_got, member(2 * q)).start()
 
-    got(rs_got, 192)
-    mine = chip_sum[chip]
-    for q in chips:
-        mine = mine + main_in[q]
+    got(rs_got, 448)
+    mine = main_send[me]
+    for peer in peers:
+        mine = mine + main_in[peer]
     main_all[chip, core] = mine
     piece = main_all.at[chip, core]
     for q in chips:
@@ -430,7 +426,7 @@
         for peer in peers:
             edge = edge + edge_in[peer]
         edge_all[chip] = edge
-        for peer in peers:
+        for peer in far_first:
             remote(edge_all.at[chip], edge_all.at[chip], edge_sent, edge_all_got, member(peer)).start()
 
     @pl.when(outer)
@@ -768,7 +764,6 @@
     wide2 = vmem(2, 2, RX, CX)
     column_c = vmem(NTR, CY, CX)
     flat = pltpu.VMEM((CY, CX), jnp.int32)
-    quarter = vmem(4, 64, CX)
     halves = vmem(4, 2, 64, CX)
     edges = vmem(NE, 8 * EB, CX)
     dma = pltpu.SemaphoreType.DMA
@@ -785,7 +780,7 @@
             vmem(7, 2, RX, CX), vmem(3, 2, RX, CX), flat, flat,
             vmem(2, 2, 64, CX), vmem(2, 2, 64, CX), vmem(2, 2, 8, CX), vmem(4, 8, CX), vmem(11 * CY, CX),
             vmem(NTR, 2, CY, CX),
-            halves, quarter, quarter, quarter, halves,
+            vmem(ND, 64, CX), vmem(ND, 64, CX), halves,
             edges, vmem(ND, 8 * EB, CX), edges,
             wide2, wide2, vmem(4, 2, RX, CX), vmem(4, 2, RX, CX),
             wide, wide, wide, wide, wide, wide, wide, wide, wide, vmem(3, 2, RX, CX),
@@ -793,7 +788,7 @@
             vmem(2, RX, CX), vmem(RX, CX), vmem(RX, CX), vmem(2, 2, CY, CX), vmem(RX, CX), vmem(2, 6, CY, CX),
             plane, plane, vmem(CY + 64, CX), vmem(CY + 64, CX),
             dma((2,)), dma, dma, dma, dma, dma, dma,
-            dma((2,)), dma, dma, dma, dma, dma, dma, dma, dma,
+            dma((2,)), dma, dma, dma, dma, dma, dma, dma,
             dma, dma, dma,
         ],
         compiler_params=pltpu.CompilerParams(

time: 32.1 us -> 32.6 us (1.016)
  Pallas kernels: 31.4 us -> 31.8 us
    pallas_call x1, Pallas kernels: 30.3 us -> 30.8 us  [body(): pl.pallas_call(kernel, out_shape=(vmem(NTR, 2, CY, CX), *(pltpu.VMEM(shap...]
where the time goes in v6:
time: 32.6 us; the launch traced here: 32.4 us
  Pallas kernels  31.8 us (98%)
  between operations  0.64 us (2%)
    pallas_call x1, Pallas kernels, body(): pl.pallas_call(kernel, out_shape=(vmem(NTR, 2, CY, CX), *(pltpu.VMEM(shap...  30.8 us
    pallas_call x1, Pallas kernels, body(): pl.pallas_call(store, out_shape=tuple((jax.ShapeDtypeStruct(shape, F32) f...  1.02 us

profile of v6, /device:TPU:35, one launch (start us, length us, event | category | flops | bytes accessed | tf_op | source)
XLA Modules:
  0.0 32.4 jit_solution(15579000399410059267)
XLA Ops:
  0.6 30.8 %shard_map.120 = (f32[6,2,128,128]{3,2,1,0:T(8,128)S(1)}, f32[1,128,128]{2,1,0:T(8,128)S(1)}, f32[1,128,128]{2,1,0:T(8,128)S(1)}, f32[1,128,128]{2,1,0:T(8,128)S...) custom-call(f32[2,1,128,128]{3,2,1,0:T(8,128)} %h_in.1, ...), custom_call_target="tpu_custom_call" | custom-call | tf_op jit(solution)/shard_map/pallas_call | solution.py:771
  31.4 1.0 %shard_map.121 = (f32[6,2,1,128,128]{4,3,2,1,0:T(8,128)}, f32[1,128,128]{2,1,0:T(8,128)}, f32[1,128,128]{2,1,0:T(8,128)}, f32[1,128,128]{2,1,0:T(8,128)}) custom-call(f32[6,2,128,128]{3,2,1,0:T(8,128)S(1)} %get-tuple-element.12.part, f32[1,128,128]{2,1,0:T(8,128)S(1)} %get-tuple-element.13.s_ref, f32[1,128,128]{2,1,0:T(8,128)S(1)} %get-tuple-element.14.e_ref, ...), custom_call_target="tpu_custom_call" | custom-call | tf_op jit(solution)/shard_map/pallas_call | solution.py:801

commit v7 on v6

--- a/solution.py
+++ b/solution.py
@@ -52,14 +52,14 @@
     x, state, wet, lev,
     side_pack, side_in, corner_pack, corner_in, sizes,
     edge_c,
-    main_send, main_in, main_all,
+    main_send, pair_in, chip_sum, main_in, main_all,
     edge_send, edge_in, edge_all,
     face_e, face_n, local, total,
     tw, ae, an, be, bn, ce, cn, wet_e_all, wet_n_all, state_b,
-    outer_send, outer_pair, outer_sum, outer_in, outer_div,
+    outer_send, outer_pair, outer_sum, outer_in, outer_next, outer_div,
     flow_n, flow_t, flow_w, flow_e, prod_n, coef, div_1, whole_div, pair_send, pair_div,
     loc_sem, sent, sent_late, edge_sent, outer_sent, up_sent, down_sent,
-    halo_got, rs_got, ag_got, forward_got, edge_got, edge_all_got, half_got, outer_got,
+    halo_got, pair_got, rs_got, ag_got, forward_got, edge_got, edge_all_got, half_got, outer_got,
     up_got, down_got, div_got,
 ):
     me = lax.axis_index("depth")
@@ -192,7 +192,8 @@
             new = [de, dn, x[2 + l, 0, here] * de, x[4 + l, 0, here] * dn]
             sums = [a + b for a, b in zip(sums, new)]
         for f in range(4):
-            main_send[p, 16 * f : 16 * f + 16] = sums[f]
+            main_send[p // 2, p % 2, 16 * f : 16 * f + 16] = sums[f]
+
     @pl.when(inner)
     def _():
         pl.semaphore_wait(barrier, 8 + ND - 1)
@@ -220,9 +221,7 @@
         halo(0, corner_pack.at[1, 0], corner_in.at[3], -1, -1)
         halo(0, x.at[:, 0, OWN : OWN + 8], x.at[:, 0, END:HIGH], 0, -1)
 
-    far_first = [(me + k) % ND for k in (4, 5, 3, 2, 6, 7, 1)]
-    for peer in far_first:
-        remote(main_send.at[peer], main_in.at[me], sent, rs_got, member(peer)).start()
+    remote(main_send.at[:, other], pair_in, sent, pair_got, member(partner)).start()
 
     fetch_c.wait()
     rows_c = slice(8, CY + 8)
@@ -244,7 +243,14 @@
 
     send_tracers(0)
 
+    got(pair_got, 256)
     chips = [(chip + k) % 4 for k in (2, 1, 3)]
+    far_first = [(me + k) % ND for k in (4, 5, 3, 2, 6, 7, 1)]
+    for q in range(4):
+        chip_sum[q] = main_send[q, core] + pair_in[q]
+    for q in chips:
+        remote(chip_sum.at[q], main_in.at[chip], sent, rs_got, member(2 * q + core)).start()
+
     def pack_more(low, shift, east, west):
         old = state[1, 0, OWN + low : OWN + low + 8]
         east = jnp.where(between(lane8, shift + 24, shift + 32), roll(old, 40 + shift, 1), east)
@@ -391,33 +397,31 @@
         for q in chips + [chip]:
             remote(edge_send.at[q], edge_in.at[me], edge_sent, edge_got, member(2 * q)).start()
 
-    got(rs_got, 448)
-    mine = main_send[me]
-    for peer in peers:
-        mine = mine + main_in[peer]
+    got(rs_got, 192)
+    mine = chip_sum[chip]
+    for q in chips:
+        mine = mine + main_in[q]
     main_all[chip, core] = mine
     piece = main_all.at[chip, core]
     for q in chips:
         remote(piece, piece, sent, ag_got, member(2 * q + core)).start()
 
-    @pl.when(outer)
-    def _():
-        for i in range(4):
-            low = OWN + 32 * i
-            here = slice(low, low + 32)
-            flux = both(local.at[2], low, 32)
-            value = flux[0] - shifted(flux, 1)[0] + local[3, 0, here] - local[3, 0, low - 1 : low + 31]
-            outer_send[i // 2, 32 * (i % 2) : 32 * (i % 2) + 32] = value
-        for j in range(2):
-            low = OWN + 64 * j
-            outer_send[j, 64:128] = local[0, 0, low : low + 64]
-            outer_send[j, 128:200] = local[1, 0, low - 8 : low + 64]
-            block = jnp.zeros((8, CX), F32)
-            for r in range(8):
-                turned = roll(local[0, 1, low + 8 * r : low + 8 * r + 8], r + 1, 1)
-                block = jnp.where(lane8 == r, turned, block)
-            outer_send[j, 200:208] = block
-        remote(outer_send, outer_pair, outer_sent, half_got, member(partner)).start()
+    for i in range(4):
+        low = OWN + 32 * i
+        here = slice(low, low + 32)
+        flux = both(local.at[2], low, 32)
+        value = flux[0] - shifted(flux, 1)[0] + local[3, 0, here] - local[3, 0, low - 1 : low + 31]
+        outer_send[i // 2, 32 * (i % 2) : 32 * (i % 2) + 32] = value
+    for j in range(2):
+        low = OWN + 64 * j
+        outer_send[j, 64:128] = local[0, 0, low : low + 64]
+        outer_send[j, 128:200] = local[1, 0, low - 8 : low + 64]
+        block = jnp.zeros((8, CX), F32)
+        for r in range(8):
+            turned = roll(local[0, 1, low + 8 * r : low + 8 * r + 8], r + 1, 1)
+            block = jnp.where(lane8 == r, turned, block)
+        outer_send[j, 200:208] = block
+    remote(outer_send, outer_pair, outer_sent, half_got, member(partner)).start()
 
     @pl.when(owner)
     def _():
@@ -569,7 +573,14 @@
         substep(state_b, state)
         return carry
 
-    lax.fori_loop(0, NSUB // 2, two, 0)
+    lax.fori_loop(0, NSUB // 2 - 1, two, 0)
+
+    @pl.when(jnp.logical_not(outer))
+    def _():
+        got(outer_got, 208)
+        remote(outer_in, outer_next, sent, div_got, member(partner)).start()
+
+    two(0, 0)
 
     flow_rows = [(OWN - 8, 8)] + [(OWN + 32 * i, 32) for i in range(4)]
     for low, size in flow_rows:
@@ -606,17 +617,15 @@
 
     @pl.when(jnp.logical_not(outer))
     def _():
-        got(outer_got, 208)
-        value = divergence_of(outer_in, pl.multiple_of(OWN + 64 * core, 8))
-        outer_div[core] = value
-        pair_send[CY : CY + 64] = value
-        remote(pair_send, pair_div, sent, div_got, member(partner)).start()
+        got(half_got, 416)
+        outer_div[core] = divergence_of(outer_in, pl.multiple_of(OWN + 64 * core, 8))
 
     @pl.when(outer)
     def _():
-        for j in range(2):
-            pair_div[64 * j : 64 * j + 64] = divergence_of(outer_pair.at[j], OWN + 64 * j)
         outer_div[...] = jnp.zeros_like(outer_div)
+
+    for j in range(2):
+        pair_div[64 * j : 64 * j + 64] = divergence_of(outer_pair.at[j], OWN + 64 * j)
 
     for low, size in flow_rows:
         here = slice(low, low + size)
@@ -674,7 +683,7 @@
 
         @pl.when(where & jnp.logical_not(outer))
         def _(rows=rows):
-            left(sent, rows + 1088)
+            left(sent, rows + 1104)
 
     @pl.when(owner)
     def _():
@@ -690,8 +699,9 @@
 
     @pl.when(jnp.logical_not(outer))
     def _():
-        got(div_got, 192)
-        outer_div[other] = pair_div[CY : CY + 64]
+        left(outer_sent, 416)
+        got(div_got, 208)
+        outer_div[other] = divergence_of(outer_next, pl.multiple_of(OWN + 64 * other, 8))
 
     odd = core == 1
     for i in range(4):
@@ -764,6 +774,7 @@
     wide2 = vmem(2, 2, RX, CX)
     column_c = vmem(NTR, CY, CX)
     flat = pltpu.VMEM((CY, CX), jnp.int32)
+    quarter = vmem(4, 64, CX)
     halves = vmem(4, 2, 64, CX)
     edges = vmem(NE, 8 * EB, CX)
     dma = pltpu.SemaphoreType.DMA
@@ -780,15 +791,15 @@
             vmem(7, 2, RX, CX), vmem(3, 2, RX, CX), flat, flat,
             vmem(2, 2, 64, CX), vmem(2, 2, 64, CX), vmem(2, 2, 8, CX), vmem(4, 8, CX), vmem(11 * CY, CX),
             vmem(NTR, 2, CY, CX),
-            vmem(ND, 64, CX), vmem(ND, 64, CX), halves,
+            halves, quarter, quarter, quarter, halves,
             edges, vmem(ND, 8 * EB, CX), edges,
             wide2, wide2, vmem(4, 2, RX, CX), vmem(4, 2, RX, CX),
             wide, wide, wide, wide, wide, wide, wide, wide, wide, vmem(3, 2, RX, CX),
-            vmem(2, 208, CX), vmem(2, 208, CX), vmem(208, CX), vmem(208, CX), vmem(2, 64, CX),
+            vmem(2, 208, CX), vmem(2, 208, CX), vmem(208, CX), vmem(208, CX), vmem(208, CX), vmem(2, 64, CX),
             vmem(2, RX, CX), vmem(RX, CX), vmem(RX, CX), vmem(2, 2, CY, CX), vmem(RX, CX), vmem(2, 6, CY, CX),
-            plane, plane, vmem(CY + 64, CX), vmem(CY + 64, CX),
+            plane, plane, plane, plane,
             dma((2,)), dma, dma, dma, dma, dma, dma,
-            dma((2,)), dma, dma, dma, dma, dma, dma, dma,
+            dma((2,)), dma, dma, dma, dma, dma, dma, dma, dma,
             dma, dma, dma,
         ],
         compiler_params=pltpu.CompilerParams(

time: 32.6 us -> 31.8 us (0.975)
  the two profiles are of different devices: /device:TPU:35 before, /device:TPU:19 now
where the time goes in v7:
time: 31.8 us; the launch traced here: 31.6 us
  Pallas kernels  31 us (97%)
  between operations  0.64 us (2%)
    pallas_call x1, Pallas kernels, body(): pl.pallas_call(kernel, out_shape=(vmem(NTR, 2, CY, CX), *(pltpu.VMEM(shap...  30 us
    pallas_call x1, Pallas kernels, body(): pl.pallas_call(store, out_shape=tuple((jax.ShapeDtypeStruct(shape, F32) f...  1.02 us

profile of v7, /device:TPU:19, one launch (start us, length us, event | category | flops | bytes accessed | tf_op | source)
XLA Modules:
  0.0 31.6 jit_solution(4903914842657648080)
XLA Ops:
  0.6 30.0 %shard_map.120 = (f32[6,2,128,128]{3,2,1,0:T(8,128)S(1)}, f32[1,128,128]{2,1,0:T(8,128)S(1)}, f32[1,128,128]{2,1,0:T(8,128)S(1)}, f32[1,128,128]{2,1,0:T(8,128)S...) custom-call(f32[2,1,128,128]{3,2,1,0:T(8,128)} %h_in.1, ...), custom_call_target="tpu_custom_call" | custom-call | tf_op jit(solution)/shard_map/pallas_call | solution.py:782
  30.6 1.0 %shard_map.121 = (f32[6,2,1,128,128]{4,3,2,1,0:T(8,128)}, f32[1,128,128]{2,1,0:T(8,128)}, f32[1,128,128]{2,1,0:T(8,128)}, f32[1,128,128]{2,1,0:T(8,128)}) custom-call(f32[6,2,128,128]{3,2,1,0:T(8,128)S(1)} %get-tuple-element.12.part, f32[1,128,128]{2,1,0:T(8,128)S(1)} %get-tuple-element.13.s_ref, f32[1,128,128]{2,1,0:T(8,128)S(1)} %get-tuple-element.14.e_ref, ...), custom_call_target="tpu_custom_call" | custom-call | tf_op jit(solution)/shard_map/pallas_call | solution.py:812

commit v8 on v7

--- a/solution.py
+++ b/solution.py
@@ -227,7 +227,7 @@
     rows_c = slice(8, CY + 8)
 
     def send_tracers(i):
-        part = slice(0, 2) if i == 0 else slice(2, NTR)
+        part = (slice(0, 3), slice(3, 4), slice(4, NTR))[i]
 
         @pl.when(me > 0)
         def _():
@@ -250,6 +250,8 @@
         chip_sum[q] = main_send[q, core] + pair_in[q]
     for q in chips:
         remote(chip_sum.at[q], main_in.at[chip], sent, rs_got, member(2 * q + core)).start()
+
+    send_tracers(1)
 
     def pack_more(low, shift, east, west):
         old = state[1, 0, OWN + low : OWN + low + 8]
@@ -440,7 +442,7 @@
         middle_chip = jnp.where(upper, 2, ND - 4)
         remote(outer_sum, outer_in, outer_sent, outer_got, member(middle_chip + core)).start()
 
-    send_tracers(1)
+    send_tracers(2)
 
     @pl.when(inner)
     def _():

time: 31.8 us -> 31.5 us (level)
  the two profiles are of different devices: /device:TPU:19 before, /device:TPU:16 now
where the time goes in v8:
time: 31.5 us; the launch traced here: 31.3 us
  Pallas kernels  30.7 us (97%)
  between operations  0.64 us (2%)
    pallas_call x1, Pallas kernels, body(): pl.pallas_call(kernel, out_shape=(vmem(NTR, 2, CY, CX), *(pltpu.VMEM(shap...  29.7 us
    pallas_call x1, Pallas kernels, body(): pl.pallas_call(store, out_shape=tuple((jax.ShapeDtypeStruct(shape, F32) f...  1.02 us

profile of v8, /device:TPU:16, one launch (start us, length us, event | category | flops | bytes accessed | tf_op | source)
XLA Modules:
  0.0 31.3 jit_solution(3013921956315072542)
XLA Ops:
  0.6 29.7 %shard_map.120 = (f32[6,2,128,128]{3,2,1,0:T(8,128)S(1)}, f32[1,128,128]{2,1,0:T(8,128)S(1)}, f32[1,128,128]{2,1,0:T(8,128)S(1)}, f32[1,128,128]{2,1,0:T(8,128)S...) custom-call(f32[2,1,128,128]{3,2,1,0:T(8,128)} %h_in.1, ...), custom_call_target="tpu_custom_call" | custom-call | tf_op jit(solution)/shard_map/pallas_call | solution.py:784
  30.3 1.0 %shard_map.121 = (f32[6,2,1,128,128]{4,3,2,1,0:T(8,128)}, f32[1,128,128]{2,1,0:T(8,128)}, f32[1,128,128]{2,1,0:T(8,128)}, f32[1,128,128]{2,1,0:T(8,128)}) custom-call(f32[6,2,128,128]{3,2,1,0:T(8,128)S(1)} %get-tuple-element.12.part, f32[1,128,128]{2,1,0:T(8,128)S(1)} %get-tuple-element.13.s_ref, f32[1,128,128]{2,1,0:T(8,128)S(1)} %get-tuple-element.14.e_ref, ...), custom_call_target="tpu_custom_call" | custom-call | tf_op jit(solution)/shard_map/pallas_call | solution.py:814

commit v9 on v8

--- a/solution.py
+++ b/solution.py
@@ -425,25 +425,6 @@
         outer_send[j, 200:208] = block
     remote(outer_send, outer_pair, outer_sent, half_got, member(partner)).start()
 
-    @pl.when(owner)
-    def _():
-        got(edge_got, 7 * 8 * EB)
-        edge = edge_send[chip]
-        for peer in peers:
-            edge = edge + edge_in[peer]
-        edge_all[chip] = edge
-        for peer in far_first:
-            remote(edge_all.at[chip], edge_all.at[chip], edge_sent, edge_all_got, member(peer)).start()
-
-    @pl.when(outer)
-    def _():
-        got(half_got, 416)
-        outer_sum[...] = outer_send[core] + outer_pair[core]
-        middle_chip = jnp.where(upper, 2, ND - 4)
-        remote(outer_sum, outer_in, outer_sent, outer_got, member(middle_chip + core)).start()
-
-    send_tracers(2)
-
     @pl.when(inner)
     def _():
         got(halo_got.at[1], 392)
@@ -488,6 +469,25 @@
             an[k, here] = (1.0 - tau) * (is_wet[k] * wet_n[k])
             wet_e_all[k, here] = (tau * coupling) * (is_wet[k] * wet_e[k])
             wet_n_all[k, here] = (tau * coupling) * (is_wet[k] * wet_n[k])
+
+    @pl.when(owner)
+    def _():
+        got(edge_got, 7 * 8 * EB)
+        edge = edge_send[chip]
+        for peer in peers:
+            edge = edge + edge_in[peer]
+        edge_all[chip] = edge
+        for peer in far_first:
+            remote(edge_all.at[chip], edge_all.at[chip], edge_sent, edge_all_got, member(peer)).start()
+
+    @pl.when(outer)
+    def _():
+        got(half_got, 416)
+        outer_sum[...] = outer_send[core] + outer_pair[core]
+        middle_chip = jnp.where(upper, 2, ND - 4)
+        remote(outer_sum, outer_in, outer_sent, outer_got, member(middle_chip + core)).start()
+
+    send_tracers(2)
 
     got(ag_got, 192)
     half = main_all.at[:, core]

time: 31.5 us -> 31.5 us (level)
  no operation moved by 1% of the time
where the time goes in v9:
time: 31.5 us; the launch traced here: 31.3 us
  Pallas kernels  30.7 us (97%)
  between operations  0.64 us (2%)
    pallas_call x1, Pallas kernels, body(): pl.pallas_call(kernel, out_shape=(vmem(NTR, 2, CY, CX), *(pltpu.VMEM(shap...  29.7 us
    pallas_call x1, Pallas kernels, body(): pl.pallas_call(store, out_shape=tuple((jax.ShapeDtypeStruct(shape, F32) f...  1.02 us

profile of v9, /device:TPU:16, one launch (start us, length us, event | category | flops | bytes accessed | tf_op | source)
XLA Modules:
  0.0 31.3 jit_solution(11699157482033373260)
XLA Ops:
  0.6 29.7 %shard_map.120 = (f32[6,2,128,128]{3,2,1,0:T(8,128)S(1)}, f32[1,128,128]{2,1,0:T(8,128)S(1)}, f32[1,128,128]{2,1,0:T(8,128)S(1)}, f32[1,128,128]{2,1,0:T(8,128)S...) custom-call(f32[2,1,128,128]{3,2,1,0:T(8,128)} %h_in.1, ...), custom_call_target="tpu_custom_call" | custom-call | tf_op jit(solution)/shard_map/pallas_call | solution.py:784
  30.3 1.0 %shard_map.121 = (f32[6,2,1,128,128]{4,3,2,1,0:T(8,128)}, f32[1,128,128]{2,1,0:T(8,128)}, f32[1,128,128]{2,1,0:T(8,128)}, f32[1,128,128]{2,1,0:T(8,128)}) custom-call(f32[6,2,128,128]{3,2,1,0:T(8,128)S(1)} %get-tuple-element.12.part, f32[1,128,128]{2,1,0:T(8,128)S(1)} %get-tuple-element.13.s_ref, f32[1,128,128]{2,1,0:T(8,128)S(1)} %get-tuple-element.14.e_ref, ...), custom_call_target="tpu_custom_call" | custom-call | tf_op jit(solution)/shard_map/pallas_call | solution.py:814
